TPU v7x, 512 devices: a whole 4x8x8 slice. The times are simulated.
512 devices in a mesh: blk: 32 (over z_hi, y, core), amp: 16 (over z_lo, x).
Axes of the slice: x: 4, y: 8, z: 8 (z_hi: 2, z_lo: 4; z = z_hi * 4 + z_lo), core: 2. Of those that a mesh axis runs over, the one named last changes fastest.
Arguments:
- amplitudes: bfloat16 [6144, 163840], P('blk', 'amp'), may hold values from -6 to 6
- integrals: bfloat16 [512, 163840], P('blk', 'amp'), may hold values from -0.02734375 to 0.02734375
- occ_pair: float32 [6144], P('blk'), may hold values from -3 to -0.5
- vir_pair: float32 [512], P('amp'), may hold values from 0.5 to 4
Outputs:
- update: float32 [6144, 512], P('blk', 'amp')
All inputs are finite; a program needn't handle non-finite values.
Results may differ from a plain program's by a relative error of at most 0.0003.
Values may be sent and summed in bfloat16 or wider, within the bound.
No kernel may reach another device: no remote copies, remote signals or barrier semaphores. Data moves between devices by JAX's collectives and lax.ppermute only.
A program may use at most 64 MiB of HBM per device.

v0:
```python
import jax
import jax.numpy as jnp
from jax import lax
from jax.sharding import PartitionSpec as P


def body(amplitudes, integrals, occ_pair, vir_pair):
    panels = lax.all_gather(integrals, "blk", axis=0, tiled=True)
    partial_value = lax.dot_general(
        amplitudes, panels, (((1,), (1,)), ((), ())), preferred_element_type=jnp.float32
    )
    portion = lax.psum_scatter(partial_value, "amp", scatter_dimension=1, tiled=True)
    return portion / (vir_pair[None, :] - occ_pair[:, None])


def solution(mesh):
    placed = (P("blk", "amp"), P("blk", "amp"), P("blk"), P("amp"))
    return jax.shard_map(
        body, mesh=mesh, in_specs=placed, out_specs=P("blk", "amp"), check_vma=False
    )
```

profile of v0, /device:TPU:24, one launch (start us, length us, event | category | flops | bytes accessed | tf_op | source)
XLA Modules:
  0.0 261.9 jit_solution(750108507096776300)
XLA Ops:
  6.5 0.0 all-gather.2.cloned.1.call-start
  6.5 0.7 all-gather.2.cloned.1.call-update
  7.3 0.0 copy-start
  7.3 0.0 copy-start.1
  7.3 0.0 reduce-scatter.2.cloned.1.call-start
  7.3 155.1 %all-gather.2.cloned.1.call-done = bf16[512,10240]{1,0:T(8,128)(2,1)} async-done(((bf16[16,10240]{1,0:T(8,128)(2,1)}), bf16[512,10240]{1,0:T(8,128)(2,1)}) %all-gather.2.cloned.1.call-update) | async-done | bytes 10485776 | tf_op jit(solution)/shard_map/all_gather | solution.py:8
  162.4 8.9 %fusion = f32[192,512]{0,1:T(8,128)} fusion(bf16[192,10240]{1,0:T(8,128)(2,1)} %param.4, bf16[512,10240]{1,0:T(8,128)(2,1)} %all-gather.2.cloned.1.call-done), kind=kOutput, calls=%fused_computation.1 | convolution fusion | flops 2013265920 | bytes 14811136 | tf_op jit(solution)/shard_map/dot_general | solution.py:9
  171.3 0.0 reduce-scatter.2.cloned.1.call-update
  171.4 82.3 %reduce-scatter.2.cloned.1.call-done = f32[192,32]{0,1:T(8,128)} async-done(((f32[192,512]{0,1:T(8,128)}), f32[192,32]{0,1:T(8,128)}) %reduce-scatter.2.cloned.1.call-update) | async-done | bytes 24592 | tf_op jit(solution)/shard_map/reduce_scatter | solution.py:12
  253.6 0.0 copy-done
  253.6 0.0 copy-done.1
  253.6 1.5 subtract_divide_fusion
Async XLA Ops:
  6.5 155.9 %all-gather.2.cloned.1.call-start = ((), (), s32[]{:S(2)}) async-start(), calls=%async_computation.1 | async-start | bytes 10813440 | tf_op jit(solution)/shard_map/all_gather | solution.py:8
  7.3 246.4 %copy-start = (f32[192]{0:T(256)S(1)}, f32[192]{0:T(256)}, u32[]{:S(2)}) copy-start(f32[192]{0:T(256)} %param.6) | copy-start | bytes 2308
  7.3 246.3 %copy-start.1 = (f32[32]{0:T(128)S(1)}, f32[32]{0:T(128)}, u32[]{:S(2)}) copy-start(f32[32]{0:T(128)} %param.7) | copy-start | bytes 388
  7.3 246.3 %reduce-scatter.2.cloned.1.call-start = ((), (), s32[]{:S(2)}) async-start(), calls=%async_computation.2 | async-start | bytes 557056 | tf_op jit(solution)/shard_map/reduce_scatter | solution.py:12
Sparse Core Ops, SparseCore 0:
  10.7 151.6 all-gather.1
  171.5 82.0 reduce-scatter.1
where the time goes:
time: 262 us
  waiting for transfers between devices  238 us (91%)
  between operations  13.4 us (5%)
  matrix products  8.88 us (3%)
    all_gather x1, waiting for transfers between devices, body(): panels = lax.all_gather(integrals, 'blk', axis=0, tiled=True)  155 us
    reduce_scatter x1, waiting for transfers between devices, body(): lax.psum_scatter(partial_value, 'amp', scatter_dimension=1, tiled=True)  82.3 us
    dot_general x1, matrix products, body(): lax.dot_general(amplitudes, panels, (((1,), (1,)), ((), ())), preferred_e...  8.88 us
  transfers between devices with their start and end apart: 2, of which 2 were waited for; matrix products, arithmetic and copies ran while one was open for 0% of the time, Pallas kernels for 0%

commit v1 on v0

v1 whole, which is shorter than its diff:
```python
import functools

import jax
import jax.numpy as jnp
from jax import lax
from jax.experimental import pallas as pl
from jax.experimental.pallas import tpu as pltpu
from jax.sharding import Mesh, PartitionSpec as P

AXES = ("zh", "y", "core", "zl", "x")
STEPS = 5


def product_kernel(keys, ny, mine, other, *refs):
    n = len(keys)
    blocks, out, acc = refs[:n], refs[n], refs[n + 1]
    rows, depth = mine.shape
    height = blocks[0].shape[0]
    kb = depth // STEPS
    for k in range(STEPS):
        cut = slice(k * kb, (k + 1) * kb)
        thin = jnp.concatenate([b[:, cut] for b in blocks], axis=0)
        for side, ref in enumerate((mine, other)):
            part = lax.dot_general(
                ref[:, cut], thin, (((1,), (1,)), ((), ())), preferred_element_type=jnp.float32
            )
            if k == 0:
                acc[side] = part
            else:
                acc[side] += part
    zh, y, core = lax.axis_index("zh"), lax.axis_index("y"), lax.axis_index("core")
    for side in range(2):
        turned = acc[side].T
        for i, (p, s) in enumerate(keys):
            home = lax.rem(zh + p, 2) * ny + lax.rem(y + s + ny, ny)
            slot = lax.rem(core + side, 2) * (2 * ny) + home
            out[pl.ds(slot, 1)] = turned[i * height : (i + 1) * height][None]


def products(keys, ny, mine, other, blocks):
    n = len(blocks)
    rows, depth = mine.shape
    height = blocks[0].shape[0]
    return pl.pallas_call(
        functools.partial(product_kernel, keys, ny),
        in_specs=[pl.BlockSpec(memory_space=pltpu.VMEM)] * (2 + n),
        out_specs=pl.BlockSpec(memory_space=pltpu.VMEM),
        out_shape=jax.ShapeDtypeStruct((2 * n, height, rows), jnp.float32),
        scratch_shapes=[pltpu.VMEM((2, rows, n * height), jnp.float32)],
        compiler_params=pltpu.CompilerParams(vmem_limit_bytes=6 * 1024 * 1024),
        cost_estimate=pl.CostEstimate(
            flops=4 * n * height * rows * depth,
            bytes_accessed=2 * (2 * rows + n * height) * depth,
            transcendentals=0,
        ),
    )(mine, other, *blocks)


def body(sizes, amplitudes, integrals, occ_pair, vir_pair):
    ny = sizes["y"]
    up = [(i, (i + 1) % ny) for i in range(ny)]
    down = [(i, (i - 1) % ny) for i in range(ny)]
    step = {1: down, -1: up}
    swap = [(0, 1), (1, 0)]
    height, rows = integrals.shape[0], amplitudes.shape[0]
    half = ny // 2

    held = {(0, 0): integrals, (1, 0): lax.ppermute(integrals, "zh", swap)}
    for s in range(1, half + 1):
        for p in range(2):
            for d in (1, -1):
                if s < half or d == (1, -1)[p]:
                    held[p, d * s] = lax.ppermute(held[p, d * (s - 1)], "y", step[d])
    other = lax.ppermute(amplitudes, "core", swap)

    keys = list(held)
    sent = products(keys, ny, amplitudes, other, [held[k] for k in keys])
    got = lax.all_to_all(sent, ("core", "zl", "x"), 0, 0, tiled=True)
    total = got.reshape(2, 2 * ny, height, rows).sum(axis=1).reshape(2 * height, rows)
    return (total / (vir_pair[:, None] - occ_pair[None, :])).T


def solution(mesh):
    blk, amp = mesh.shape["blk"], mesh.shape["amp"]
    sizes = {"zh": 2, "y": blk // 4, "core": 2, "zl": 4, "x": amp // 4}
    fine = Mesh(mesh.devices.reshape(tuple(sizes[a] for a in AXES)), AXES)
    b, a = ("zh", "y", "core"), ("zl", "x")
    return jax.shard_map(
        functools.partial(body, sizes),
        mesh=fine,
        in_specs=(P(b, a), P(b, a), P(b), P(a)),
        out_specs=P(b, a),
        check_vma=False,
    )
```

time: 262 us -> 117 us (0.45)
  the two profiles are of different devices: /device:TPU:24 before, /device:TPU:1 now
where the time goes in v1:
time: 117 us; the launch traced here: 116 us
  starting transfers between devices  56.3 us (48%)
  blocking collectives  29.7 us (25%)
  waiting for transfers between devices  22.6 us (19%)
  Pallas kernels  3.75 us (3%)
  local copies, waits for them, and re-layouts  3.09 us (3%)
    ppermute x14, starting transfers between devices, body(): held[p, d * s] = lax.ppermute(held[p, d * (s - 1)], 'y', step[d])  42.3 us
    all_to_all x1, blocking collectives, body(): got = lax.all_to_all(sent, ('core', 'zl', 'x'), 0, 0, tiled=True)  29.7 us
    ppermute x14, waiting for transfers between devices, body(): held[p, d * s] = lax.ppermute(held[p, d * (s - 1)], 'y', step[d])  13.8 us
    ppermute x1, waiting for transfers between devices, body(): held = {(0, 0): integrals, (1, 0): lax.ppermute(integrals, 'zh', swap)}  8.78 us
    ppermute x1, starting transfers between devices, body(): other = lax.ppermute(amplitudes, 'core', swap)  8.77 us
    ppermute x1, starting transfers between devices, body(): held = {(0, 0): integrals, (1, 0): lax.ppermute(integrals, 'zh', swap)}  5.26 us
    pallas_call x1, Pallas kernels, products(): pl.pallas_call(functools.partial(product_kernel, keys, ny), in_specs=[pl....  3.75 us
    unnamed x8, local copies, waits for them, and re-layouts  3.09 us
  transfers between devices with their start and end apart: 16, of which 6 were waited for; matrix products, arithmetic and copies ran while one was open for 0% of the time, Pallas kernels for 0%

profile of v1, /device:TPU:1, one launch (start us, length us, event | category | flops | bytes accessed | tf_op | source)
XLA Modules:
  0.0 116.4 jit_solution(290015790898037080)
XLA Ops:
  0.0 8.8 %collective-permute-start = (bf16[192,10240]{1,0:T(8,128)(2,1)}, bf16[192,10240]{1,0:T(8,128)(2,1)S(1)}, u32[]{:S(2)}, u32[]{:S(2)}) collective-permute-start(bf16[192,10240]{1,0:T(8,128)(2,1)} %mine.1), channel_id=1, source_target_pairs={{0,16},{16,0},{1,17},{17,1},{2,18},{18,2},{3,19},{19,3},{4,20},{20... | collective-permute-start | bytes 11796488 | tf_op jit(solution)/shard_map/ppermute | solution.py:74
  8.8 5.3 %collective-permute-start.1 = (bf16[16,10240]{1,0:T(8,128)(2,1)}, bf16[16,10240]{1,0:T(8,128)(2,1)S(1)}, u32[]{:S(2)}, u32[]{:S(2)}) collective-permute-start(bf16[16,10240]{1,0:T(8,128)(2,1)} %refs_0_.1), channel_id=1, source_target_pairs={{0,256},{256,0},{1,257},{257,1},{2,258},{258,2},{3,259},{259,3},{4... | collective-permute-start | bytes 983048 | tf_op jit(solution)/shard_map/ppermute | solution.py:68
  14.1 5.1 %collective-permute-start.2 = (bf16[16,10240]{1,0:T(8,128)(2,1)}, bf16[16,10240]{1,0:T(8,128)(2,1)S(1)}, u32[]{:S(2)}, u32[]{:S(2)}) collective-permute-start(bf16[16,10240]{1,0:T(8,128)(2,1)} %refs_0_.1), channel_id=1, source_target_pairs={{0,224},{32,0},{64,32},{96,64},{128,96},{160,128},{192,160},{224,1... | collective-permute-start | bytes 983048 | tf_op jit(solution)/shard_map/ppermute | solution.py:73
  19.2 8.8 %collective-permute-done.1.refs_1_ = bf16[16,10240]{1,0:T(8,128)(2,1)S(1)} collective-permute-done((bf16[16,10240]{1,0:T(8,128)(2,1)}, bf16[16,10240]{1,0:T(8,128)(2,1)S(1)}, u32[]{:S(2)}, u32[]{:S(2)}) %collective-permute-start.1) | collective-permute-done | bytes 327712 | tf_op jit(solution)/shard_map/ppermute | solution.py:68
  27.9 1.9 %collective-permute-start.5 = (bf16[16,10240]{1,0:T(8,128)(2,1)S(1)}, bf16[16,10240]{1,0:T(8,128)(2,1)S(1)}, u32[]{:S(2)}, u32[]{:S(2)}) collective-permute-start(bf16[16,10240]{1,0:T(8,128)(2,1)S(1)} %collective-permute-done.1.refs_1_), channel_id=1, source_target_pairs={{0,32},{32,64},{64,96},{96,128},{128,160},{160,192},{192,224},{224... | collective-permute-start | bytes 983048 | tf_op jit(solution)/shard_map/ppermute | solution.py:73
  29.9 1.9 %collective-permute-start.3 = (bf16[16,10240]{1,0:T(8,128)(2,1)}, bf16[16,10240]{1,0:T(8,128)(2,1)S(1)}, u32[]{:S(2)}, u32[]{:S(2)}) collective-permute-start(bf16[16,10240]{1,0:T(8,128)(2,1)} %refs_0_.1), channel_id=1, source_target_pairs={{0,32},{32,64},{64,96},{96,128},{128,160},{160,192},{192,224},{224... | collective-permute-start | bytes 983048 | tf_op jit(solution)/shard_map/ppermute | solution.py:73
  31.8 4.6 %collective-permute-start.6 = (bf16[16,10240]{1,0:T(8,128)(2,1)S(1)}, bf16[16,10240]{1,0:T(8,128)(2,1)S(1)}, u32[]{:S(2)}, u32[]{:S(2)}) collective-permute-start(bf16[16,10240]{1,0:T(8,128)(2,1)S(1)} %collective-permute-done.2.refs_2_), channel_id=1, source_target_pairs={{0,224},{32,0},{64,32},{96,64},{128,96},{160,128},{192,160},{224,1... | collective-permute-start | bytes 983048 | tf_op jit(solution)/shard_map/ppermute | solution.py:73
  36.4 3.4 %collective-permute-start.4 = (bf16[16,10240]{1,0:T(8,128)(2,1)S(1)}, bf16[16,10240]{1,0:T(8,128)(2,1)S(1)}, u32[]{:S(2)}, u32[]{:S(2)}) collective-permute-start(bf16[16,10240]{1,0:T(8,128)(2,1)S(1)} %collective-permute-done.1.refs_1_), channel_id=1, source_target_pairs={{0,224},{32,0},{64,32},{96,64},{128,96},{160,128},{192,160},{224,1... | collective-permute-start | bytes 983048 | tf_op jit(solution)/shard_map/ppermute | solution.py:73
  39.7 0.0 collective-permute-done.5.refs_5_
  39.8 1.9 %collective-permute-start.9 = (bf16[16,10240]{1,0:T(8,128)(2,1)S(1)}, bf16[16,10240]{1,0:T(8,128)(2,1)S(1)}, u32[]{:S(2)}, u32[]{:S(2)}) collective-permute-start(bf16[16,10240]{1,0:T(8,128)(2,1)S(1)} %collective-permute-done.5.refs_5_), channel_id=1, source_target_pairs={{0,32},{32,64},{64,96},{96,128},{128,160},{160,192},{192,224},{224... | collective-permute-start | bytes 983048 | tf_op jit(solution)/shard_map/ppermute | solution.py:73
  41.7 4.6 %collective-permute-done.3.refs_3_ = bf16[16,10240]{1,0:T(8,128)(2,1)S(1)} collective-permute-done((bf16[16,10240]{1,0:T(8,128)(2,1)}, bf16[16,10240]{1,0:T(8,128)(2,1)S(1)}, u32[]{:S(2)}, u32[]{:S(2)}) %collective-permute-start.3) | collective-permute-done | bytes 327712 | tf_op jit(solution)/shard_map/ppermute | solution.py:73
  46.3 1.9 %collective-permute-start.7 = (bf16[16,10240]{1,0:T(8,128)(2,1)S(1)}, bf16[16,10240]{1,0:T(8,128)(2,1)S(1)}, u32[]{:S(2)}, u32[]{:S(2)}) collective-permute-start(bf16[16,10240]{1,0:T(8,128)(2,1)S(1)} %collective-permute-done.3.refs_3_), channel_id=1, source_target_pairs={{0,32},{32,64},{64,96},{96,128},{128,160},{160,192},{192,224},{224... | collective-permute-start | bytes 983048 | tf_op jit(solution)/shard_map/ppermute | solution.py:73
  48.3 0.0 collective-permute-done.6.refs_6_
  48.3 4.6 %collective-permute-start.10 = (bf16[16,10240]{1,0:T(8,128)(2,1)S(1)}, bf16[16,10240]{1,0:T(8,128)(2,1)S(1)}, u32[]{:S(2)}, u32[]{:S(2)}) collective-permute-start(bf16[16,10240]{1,0:T(8,128)(2,1)S(1)} %collective-permute-done.6.refs_6_), channel_id=1, source_target_pairs={{0,224},{32,0},{64,32},{96,64},{128,96},{160,128},{192,160},{224,1... | collective-permute-start | bytes 983048 | tf_op jit(solution)/shard_map/ppermute | solution.py:73
  52.9 1.9 %collective-permute-start.8 = (bf16[16,10240]{1,0:T(8,128)(2,1)S(1)}, bf16[16,10240]{1,0:T(8,128)(2,1)S(1)}, u32[]{:S(2)}, u32[]{:S(2)}) collective-permute-start(bf16[16,10240]{1,0:T(8,128)(2,1)S(1)} %collective-permute-done.4.refs_4_), channel_id=1, source_target_pairs={{0,224},{32,0},{64,32},{96,64},{128,96},{160,128},{192,160},{224,1... | collective-permute-start | bytes 983048 | tf_op jit(solution)/shard_map/ppermute | solution.py:73
  54.8 0.0 collective-permute-done.9.refs_9_
  54.8 3.4 %collective-permute-start.13 = (bf16[16,10240]{1,0:T(8,128)(2,1)S(1)}, bf16[16,10240]{1,0:T(8,128)(2,1)S(1)}, u32[]{:S(2)}, u32[]{:S(2)}) collective-permute-start(bf16[16,10240]{1,0:T(8,128)(2,1)S(1)} %collective-permute-done.9.refs_9_), channel_id=1, source_target_pairs={{0,32},{32,64},{64,96},{96,128},{128,160},{160,192},{192,224},{224... | collective-permute-start | bytes 983048 | tf_op jit(solution)/shard_map/ppermute | solution.py:73
  58.2 2.2 %collective-permute-done.7.refs_7_ = bf16[16,10240]{1,0:T(8,128)(2,1)S(1)} collective-permute-done((bf16[16,10240]{1,0:T(8,128)(2,1)S(1)}, bf16[16,10240]{1,0:T(8,128)(2,1)S(1)}, u32[]{:S(2)}, u32[]{:S(2)}) %collective-permute-start.7) | collective-permute-done | bytes 327712 | tf_op jit(solution)/shard_map/ppermute | solution.py:73
  60.4 1.9 %collective-permute-start.11 = (bf16[16,10240]{1,0:T(8,128)(2,1)S(1)}, bf16[16,10240]{1,0:T(8,128)(2,1)S(1)}, u32[]{:S(2)}, u32[]{:S(2)}) collective-permute-start(bf16[16,10240]{1,0:T(8,128)(2,1)S(1)} %collective-permute-done.7.refs_7_), channel_id=1, source_target_pairs={{0,32},{32,64},{64,96},{96,128},{128,160},{160,192},{192,224},{224... | collective-permute-start | bytes 983048 | tf_op jit(solution)/shard_map/ppermute | solution.py:73
  62.3 4.6 %collective-permute-start.14 = (bf16[16,10240]{1,0:T(8,128)(2,1)S(1)}, bf16[16,10240]{1,0:T(8,128)(2,1)S(1)}, u32[]{:S(2)}, u32[]{:S(2)}) collective-permute-start(bf16[16,10240]{1,0:T(8,128)(2,1)S(1)} %collective-permute-done.10.refs_10_), channel_id=1, source_target_pairs={{0,224},{32,0},{64,32},{96,64},{128,96},{160,128},{192,160},{224,1... | collective-permute-start | bytes 983048 | tf_op jit(solution)/shard_map/ppermute | solution.py:73
  66.9 0.0 collective-permute-done.8.refs_8_
  66.9 1.9 %collective-permute-start.12 = (bf16[16,10240]{1,0:T(8,128)(2,1)S(1)}, bf16[16,10240]{1,0:T(8,128)(2,1)S(1)}, u32[]{:S(2)}, u32[]{:S(2)}) collective-permute-start(bf16[16,10240]{1,0:T(8,128)(2,1)S(1)} %collective-permute-done.8.refs_8_), channel_id=1, source_target_pairs={{0,224},{32,0},{64,32},{96,64},{128,96},{160,128},{192,160},{224,1... | collective-permute-start | bytes 983048 | tf_op jit(solution)/shard_map/ppermute | solution.py:73
  68.8 3.4 %collective-permute-start.15 = (bf16[16,10240]{1,0:T(8,128)(2,1)S(1)}, bf16[16,10240]{1,0:T(8,128)(2,1)S(1)}, u32[]{:S(2)}, u32[]{:S(2)}) collective-permute-start(bf16[16,10240]{1,0:T(8,128)(2,1)S(1)} %collective-permute-done.13.refs_13_), channel_id=1, source_target_pairs={{0,32},{32,64},{64,96},{96,128},{128,160},{160,192},{192,224},{224... | collective-permute-start | bytes 983048 | tf_op jit(solution)/shard_map/ppermute | solution.py:73
  72.2 1.0 collective-permute-done.11.refs_11_
  73.2 0.0 collective-permute-done.14.refs_14_
  73.2 5.3 %collective-permute-done.12.refs_12_ = bf16[16,10240]{1,0:T(8,128)(2,1)S(1)} collective-permute-done((bf16[16,10240]{1,0:T(8,128)(2,1)S(1)}, bf16[16,10240]{1,0:T(8,128)(2,1)S(1)}, u32[]{:S(2)}, u32[]{:S(2)}) %collective-permute-start.12) | collective-permute-done | bytes 327712 | tf_op jit(solution)/shard_map/ppermute | solution.py:73
  78.5 0.6 collective-permute-done.15.refs_15_
  79.1 2.1 %copy-done = bf16[192,10240]{1,0:T(8,128)(2,1)S(1)} copy-done((bf16[192,10240]{1,0:T(8,128)(2,1)S(1)}, bf16[192,10240]{1,0:T(8,128)(2,1)}, u32[]{:S(2)}) %copy-start) | copy-done | bytes 3932184
  81.2 1.0 copy-done.1
  82.2 3.7 %shard_map.46 = f32[32,16,192]{2,1,0:T(8,128)S(1)} custom-call(bf16[192,10240]{1,0:T(8,128)(2,1)S(1)} %copy-done, bf16[192,10240]{1,0:T(8,128)(2,1)S(1)} %collective-permute-done.other, bf16[16,10240]{1,0:T(8,128)(2,1)S(1)} %copy-done.1, bf16[16,10240]{1,0:T(8,128)(2,1)S(1)} %collective-permute-done.1.refs_1_, ...), custom_call_target="tpu_custom_call" | custom-call | flops 2013265920 | bytes 13107200 | tf_op jit(solution)/shard_map/pallas_call | solution.py:44
  85.9 29.7 %all_to_all.5 = f32[32,16,192]{2,1,0:T(8,128)S(1)} all-to-all(f32[32,16,192]{2,1,0:T(8,128)S(1)} %shard_map.46), channel_id=1, replica_groups=mesh['zh'=2,'y'=8,'core'=2,'zl'=4,'x'=4] {'core','zl','x'}, dimensions={0} | all-to-all | bytes 786432 | tf_op jit(solution)/shard_map/all_to_all | solution.py:78
  115.7 0.7 bitcast_divide_fusion
  (12 shorter events, 0.1 us)
Async XLA Ops:
  0.0 79.1 %collective-permute-start = (bf16[192,10240]{1,0:T(8,128)(2,1)}, bf16[192,10240]{1,0:T(8,128)(2,1)S(1)}, u32[]{:S(2)}, u32[]{:S(2)}) collective-permute-start(bf16[192,10240]{1,0:T(8,128)(2,1)} %mine.1), channel_id=1, source_target_pairs={{0,16},{16,0},{1,17},{17,1},{2,18},{18,2},{3,19},{19,3},{4,20},{20... | collective-permute-start | bytes 11796488 | tf_op jit(solution)/shard_map/ppermute | solution.py:74
  8.8 19.2 %collective-permute-start.1 = (bf16[16,10240]{1,0:T(8,128)(2,1)}, bf16[16,10240]{1,0:T(8,128)(2,1)S(1)}, u32[]{:S(2)}, u32[]{:S(2)}) collective-permute-start(bf16[16,10240]{1,0:T(8,128)(2,1)} %refs_0_.1), channel_id=1, source_target_pairs={{0,256},{256,0},{1,257},{257,1},{2,258},{258,2},{3,259},{259,3},{4... | collective-permute-start | bytes 983048 | tf_op jit(solution)/shard_map/ppermute | solution.py:68
  14.1 17.7 %collective-permute-start.2 = (bf16[16,10240]{1,0:T(8,128)(2,1)}, bf16[16,10240]{1,0:T(8,128)(2,1)S(1)}, u32[]{:S(2)}, u32[]{:S(2)}) collective-permute-start(bf16[16,10240]{1,0:T(8,128)(2,1)} %refs_0_.1), channel_id=1, source_target_pairs={{0,224},{32,0},{64,32},{96,64},{128,96},{160,128},{192,160},{224,1... | collective-permute-start | bytes 983048 | tf_op jit(solution)/shard_map/ppermute | solution.py:73
  27.9 11.8 %collective-permute-start.5 = (bf16[16,10240]{1,0:T(8,128)(2,1)S(1)}, bf16[16,10240]{1,0:T(8,128)(2,1)S(1)}, u32[]{:S(2)}, u32[]{:S(2)}) collective-permute-start(bf16[16,10240]{1,0:T(8,128)(2,1)S(1)} %collective-permute-done.1.refs_1_), channel_id=1, source_target_pairs={{0,32},{32,64},{64,96},{96,128},{128,160},{160,192},{192,224},{224... | collective-permute-start | bytes 983048 | tf_op jit(solution)/shard_map/ppermute | solution.py:73
  29.9 16.5 %collective-permute-start.3 = (bf16[16,10240]{1,0:T(8,128)(2,1)}, bf16[16,10240]{1,0:T(8,128)(2,1)S(1)}, u32[]{:S(2)}, u32[]{:S(2)}) collective-permute-start(bf16[16,10240]{1,0:T(8,128)(2,1)} %refs_0_.1), channel_id=1, source_target_pairs={{0,32},{32,64},{64,96},{96,128},{128,160},{160,192},{192,224},{224... | collective-permute-start | bytes 983048 | tf_op jit(solution)/shard_map/ppermute | solution.py:73
  31.8 16.5 %collective-permute-start.6 = (bf16[16,10240]{1,0:T(8,128)(2,1)S(1)}, bf16[16,10240]{1,0:T(8,128)(2,1)S(1)}, u32[]{:S(2)}, u32[]{:S(2)}) collective-permute-start(bf16[16,10240]{1,0:T(8,128)(2,1)S(1)} %collective-permute-done.2.refs_2_), channel_id=1, source_target_pairs={{0,224},{32,0},{64,32},{96,64},{128,96},{160,128},{192,160},{224,1... | collective-permute-start | bytes 983048 | tf_op jit(solution)/shard_map/ppermute | solution.py:73
  36.4 16.5 %collective-permute-start.4 = (bf16[16,10240]{1,0:T(8,128)(2,1)S(1)}, bf16[16,10240]{1,0:T(8,128)(2,1)S(1)}, u32[]{:S(2)}, u32[]{:S(2)}) collective-permute-start(bf16[16,10240]{1,0:T(8,128)(2,1)S(1)} %collective-permute-done.1.refs_1_), channel_id=1, source_target_pairs={{0,224},{32,0},{64,32},{96,64},{128,96},{160,128},{192,160},{224,1... | collective-permute-start | bytes 983048 | tf_op jit(solution)/shard_map/ppermute | solution.py:73
  39.8 15.0 %collective-permute-start.9 = (bf16[16,10240]{1,0:T(8,128)(2,1)S(1)}, bf16[16,10240]{1,0:T(8,128)(2,1)S(1)}, u32[]{:S(2)}, u32[]{:S(2)}) collective-permute-start(bf16[16,10240]{1,0:T(8,128)(2,1)S(1)} %collective-permute-done.5.refs_5_), channel_id=1, source_target_pairs={{0,32},{32,64},{64,96},{96,128},{128,160},{160,192},{192,224},{224... | collective-permute-start | bytes 983048 | tf_op jit(solution)/shard_map/ppermute | solution.py:73
  46.3 14.0 %collective-permute-start.7 = (bf16[16,10240]{1,0:T(8,128)(2,1)S(1)}, bf16[16,10240]{1,0:T(8,128)(2,1)S(1)}, u32[]{:S(2)}, u32[]{:S(2)}) collective-permute-start(bf16[16,10240]{1,0:T(8,128)(2,1)S(1)} %collective-permute-done.3.refs_3_), channel_id=1, source_target_pairs={{0,32},{32,64},{64,96},{96,128},{128,160},{160,192},{192,224},{224... | collective-permute-start | bytes 983048 | tf_op jit(solution)/shard_map/ppermute | solution.py:73
  48.3 14.0 %collective-permute-start.10 = (bf16[16,10240]{1,0:T(8,128)(2,1)S(1)}, bf16[16,10240]{1,0:T(8,128)(2,1)S(1)}, u32[]{:S(2)}, u32[]{:S(2)}) collective-permute-start(bf16[16,10240]{1,0:T(8,128)(2,1)S(1)} %collective-permute-done.6.refs_6_), channel_id=1, source_target_pairs={{0,224},{32,0},{64,32},{96,64},{128,96},{160,128},{192,160},{224,1... | collective-permute-start | bytes 983048 | tf_op jit(solution)/shard_map/ppermute | solution.py:73
  52.9 14.0 %collective-permute-start.8 = (bf16[16,10240]{1,0:T(8,128)(2,1)S(1)}, bf16[16,10240]{1,0:T(8,128)(2,1)S(1)}, u32[]{:S(2)}, u32[]{:S(2)}) collective-permute-start(bf16[16,10240]{1,0:T(8,128)(2,1)S(1)} %collective-permute-done.4.refs_4_), channel_id=1, source_target_pairs={{0,224},{32,0},{64,32},{96,64},{128,96},{160,128},{192,160},{224,1... | collective-permute-start | bytes 983048 | tf_op jit(solution)/shard_map/ppermute | solution.py:73
  54.8 14.0 %collective-permute-start.13 = (bf16[16,10240]{1,0:T(8,128)(2,1)S(1)}, bf16[16,10240]{1,0:T(8,128)(2,1)S(1)}, u32[]{:S(2)}, u32[]{:S(2)}) collective-permute-start(bf16[16,10240]{1,0:T(8,128)(2,1)S(1)} %collective-permute-done.9.refs_9_), channel_id=1, source_target_pairs={{0,32},{32,64},{64,96},{96,128},{128,160},{160,192},{192,224},{224... | collective-permute-start | bytes 983048 | tf_op jit(solution)/shard_map/ppermute | solution.py:73
  60.4 12.9 %collective-permute-start.11 = (bf16[16,10240]{1,0:T(8,128)(2,1)S(1)}, bf16[16,10240]{1,0:T(8,128)(2,1)S(1)}, u32[]{:S(2)}, u32[]{:S(2)}) collective-permute-start(bf16[16,10240]{1,0:T(8,128)(2,1)S(1)} %collective-permute-done.7.refs_7_), channel_id=1, source_target_pairs={{0,32},{32,64},{64,96},{96,128},{128,160},{160,192},{192,224},{224... | collective-permute-start | bytes 983048 | tf_op jit(solution)/shard_map/ppermute | solution.py:73
  62.3 10.9 %collective-permute-start.14 = (bf16[16,10240]{1,0:T(8,128)(2,1)S(1)}, bf16[16,10240]{1,0:T(8,128)(2,1)S(1)}, u32[]{:S(2)}, u32[]{:S(2)}) collective-permute-start(bf16[16,10240]{1,0:T(8,128)(2,1)S(1)} %collective-permute-done.10.refs_10_), channel_id=1, source_target_pairs={{0,224},{32,0},{64,32},{96,64},{128,96},{160,128},{192,160},{224,1... | collective-permute-start | bytes 983048 | tf_op jit(solution)/shard_map/ppermute | solution.py:73
  66.9 11.6 %collective-permute-start.12 = (bf16[16,10240]{1,0:T(8,128)(2,1)S(1)}, bf16[16,10240]{1,0:T(8,128)(2,1)S(1)}, u32[]{:S(2)}, u32[]{:S(2)}) collective-permute-start(bf16[16,10240]{1,0:T(8,128)(2,1)S(1)} %collective-permute-done.8.refs_8_), channel_id=1, source_target_pairs={{0,224},{32,0},{64,32},{96,64},{128,96},{160,128},{192,160},{224,1... | collective-permute-start | bytes 983048 | tf_op jit(solution)/shard_map/ppermute | solution.py:73
  68.8 10.3 %collective-permute-start.15 = (bf16[16,10240]{1,0:T(8,128)(2,1)S(1)}, bf16[16,10240]{1,0:T(8,128)(2,1)S(1)}, u32[]{:S(2)}, u32[]{:S(2)}) collective-permute-start(bf16[16,10240]{1,0:T(8,128)(2,1)S(1)} %collective-permute-done.13.refs_13_), channel_id=1, source_target_pairs={{0,32},{32,64},{64,96},{96,128},{128,160},{160,192},{192,224},{224... | collective-permute-start | bytes 983048 | tf_op jit(solution)/shard_map/ppermute | solution.py:73
  79.1 2.1 %copy-start = (bf16[192,10240]{1,0:T(8,128)(2,1)S(1)}, bf16[192,10240]{1,0:T(8,128)(2,1)}, u32[]{:S(2)}) copy-start(bf16[192,10240]{1,0:T(8,128)(2,1)} %mine.1) | copy-start | bytes 11796484
  81.2 1.0 copy-start.1
  82.2 33.5 %copy-start.2 = (f32[192]{0:T(256)S(1)}, f32[192]{0:T(256)}, u32[]{:S(2)}) copy-start(f32[192]{0:T(256)} %param.6) | copy-start | bytes 2308
  82.2 33.5 %copy-start.3 = (f32[32]{0:T(128)S(1)}, f32[32]{0:T(128)}, u32[]{:S(2)}) copy-start(f32[32]{0:T(128)} %param.7) | copy-start | bytes 388

commit v2 on v1

--- a/solution.py
+++ b/solution.py
@@ -9,6 +9,7 @@
 
 AXES = ("zh", "y", "core", "zl", "x")
 STEPS = 5
+LANES = 128
 
 
 def product_kernel(keys, ny, mine, other, *refs):
@@ -29,12 +30,41 @@
             else:
                 acc[side] += part
     zh, y, core = lax.axis_index("zh"), lax.axis_index("y"), lax.axis_index("core")
+    half = height // 2
     for side in range(2):
         turned = acc[side].T
         for i, (p, s) in enumerate(keys):
-            home = lax.rem(zh + p, 2) * ny + lax.rem(y + s + ny, ny)
+            home = lax.rem(zh + p, 2) * ny + lax.rem(y + s * (1 - 2 * core) + ny, ny)
             slot = lax.rem(core + side, 2) * (2 * ny) + home
-            out[pl.ds(slot, 1)] = turned[i * height : (i + 1) * height][None]
+            tile = turned[i * height : (i + 1) * height]
+            out[pl.ds(slot, 1), :height] = tile[None, :, :LANES]
+            rest = jnp.concatenate([tile[:half, LANES:], tile[half:, LANES:]], axis=1)
+            out[pl.ds(slot, 1), height:] = rest[None]
+
+
+def fetch_kernel(mine, own, mine_near, own_near, sems):
+    copies = [
+        pltpu.make_async_copy(mine, mine_near, sems.at[0]),
+        pltpu.make_async_copy(own, own_near, sems.at[1]),
+    ]
+    for copy in copies:
+        copy.start()
+    for copy in copies:
+        copy.wait()
+
+
+def fetch(mine, own):
+    return pl.pallas_call(
+        fetch_kernel,
+        in_specs=[pl.BlockSpec(memory_space=pl.ANY)] * 2,
+        out_specs=[pl.BlockSpec(memory_space=pltpu.VMEM)] * 2,
+        out_shape=[jax.ShapeDtypeStruct(a.shape, a.dtype) for a in (mine, own)],
+        scratch_shapes=[pltpu.SemaphoreType.DMA((2,))],
+        compiler_params=pltpu.CompilerParams(vmem_limit_bytes=2 * 1024 * 1024),
+        cost_estimate=pl.CostEstimate(
+            flops=0, bytes_accessed=4 * (mine.size + own.size), transcendentals=0
+        ),
+    )(mine, own)
 
 
 def products(keys, ny, mine, other, blocks):
@@ -45,9 +75,9 @@
         functools.partial(product_kernel, keys, ny),
         in_specs=[pl.BlockSpec(memory_space=pltpu.VMEM)] * (2 + n),
         out_specs=pl.BlockSpec(memory_space=pltpu.VMEM),
-        out_shape=jax.ShapeDtypeStruct((2 * n, height, rows), jnp.float32),
+        out_shape=jax.ShapeDtypeStruct((2 * n, height * rows // LANES, LANES), jnp.float32),
         scratch_shapes=[pltpu.VMEM((2, rows, n * height), jnp.float32)],
-        compiler_params=pltpu.CompilerParams(vmem_limit_bytes=6 * 1024 * 1024),
+        compiler_params=pltpu.CompilerParams(vmem_limit_bytes=8 * 1024 * 1024),
         cost_estimate=pl.CostEstimate(
             flops=4 * n * height * rows * depth,
             bytes_accessed=2 * (2 * rows + n * height) * depth,
@@ -58,25 +88,36 @@
 
 def body(sizes, amplitudes, integrals, occ_pair, vir_pair):
     ny = sizes["y"]
-    up = [(i, (i + 1) % ny) for i in range(ny)]
-    down = [(i, (i - 1) % ny) for i in range(ny)]
-    step = {1: down, -1: up}
     swap = [(0, 1), (1, 0)]
     height, rows = integrals.shape[0], amplitudes.shape[0]
-    half = ny // 2
+    tie = lax.optimization_barrier
 
-    held = {(0, 0): integrals, (1, 0): lax.ppermute(integrals, "zh", swap)}
-    for s in range(1, half + 1):
-        for p in range(2):
-            for d in (1, -1):
-                if s < half or d == (1, -1)[p]:
-                    held[p, d * s] = lax.ppermute(held[p, d * (s - 1)], "y", step[d])
+    def hop(block, away):
+        pairs = [(2 * i + c, 2 * ((i - away * (1 - 2 * c)) % ny) + c) for i in range(ny) for c in range(2)]
+        return lax.ppermute(block, ("y", "core"), pairs)
+
+    near, far = {0: integrals}, {0: lax.ppermute(integrals, "zh", swap)}
+    for s in (1, 2, 3):
+        near[s], near[-s] = hop(near[s - 1], 1), hop(near[1 - s], -1)
+    near[4] = hop(near[3], 1)
     other = lax.ppermute(amplitudes, "core", swap)
+    for s in (1, 2):
+        far[s], far[-s] = hop(far[s - 1], 1), hop(far[1 - s], -1)
+    far[3] = hop(far[2], 1)
+    last, near[-3] = tie((far[-2], near[-3]))
+    far[-3] = hop(last, -1)
+    last, near[4], near[-3] = tie((far[3], near[4], near[-3]))
+    far[4] = hop(last, 1)
 
+    held = {(p, s): block for p, plane in enumerate((near, far)) for s, block in plane.items()}
+    mine, held[0, 0] = fetch(amplitudes, integrals)
     keys = list(held)
-    sent = products(keys, ny, amplitudes, other, [held[k] for k in keys])
+    sent = products(keys, ny, mine, other, [held[k] for k in keys])
     got = lax.all_to_all(sent, ("core", "zl", "x"), 0, 0, tiled=True)
-    total = got.reshape(2, 2 * ny, height, rows).sum(axis=1).reshape(2 * height, rows)
+    total = got.reshape(2, 2 * ny, -1, LANES).sum(axis=1)
+    left, rest = total[:, :height], total[:, height:]
+    right = jnp.concatenate([rest[..., : rows - LANES], rest[..., rows - LANES :]], axis=1)
+    total = jnp.concatenate([left, right], axis=2).reshape(2 * height, rows)
     return (total / (vir_pair[:, None] - occ_pair[None, :])).T
 
 

time: 117 us -> 108 us (0.923)
  waiting for transfers between devices: 22.6 us -> 9.47 us
  starting transfers between devices: 56.3 us -> 63.7 us
  blocking collectives: 29.7 us -> 25.3 us
    ppermute x15, waiting for transfers between devices: 22.6 us -> 9.47 us  [the longest x14 7.12 us: hop(): return lax.ppermute(block, ('y', 'core'), pairs)]
    ppermute x15, starting transfers between devices: 47.6 us -> 55 us  [the longest x14 48.4 us: hop(): return lax.ppermute(block, ('y', 'core'), pairs)]
    all_to_all x1, blocking collectives: 29.7 us -> 25.3 us  [body(): got = lax.all_to_all(sent, ('core', 'zl', 'x'), 0, 0, tiled=True)]
  transfers between devices with their start and end apart: 16 -> 16, of which waited for: 6 -> 5; matrix products, arithmetic and copies ran while one was open for 0% -> 0% of each run, Pallas kernels for 0% -> 0%
where the time goes in v2:
time: 108 us; the launch traced here: 107 us
  starting transfers between devices  63.7 us (59%)
  blocking collectives  25.3 us (23%)
  waiting for transfers between devices  9.47 us (9%)
  Pallas kernels  4.21 us (4%)
  local copies, waits for them, and re-layouts  3.16 us (3%)
    ppermute x14, starting transfers between devices, hop(): return lax.ppermute(block, ('y', 'core'), pairs)  48.4 us
    all_to_all x1, blocking collectives, body(): got = lax.all_to_all(sent, ('core', 'zl', 'x'), 0, 0, tiled=True)  25.3 us
    ppermute x1, starting transfers between devices, body(): other = lax.ppermute(amplitudes, 'core', swap)  8.77 us
    ppermute x14, waiting for transfers between devices, hop(): return lax.ppermute(block, ('y', 'core'), pairs)  7.12 us
    ppermute x1, starting transfers between devices, body(): near, far = ({0: integrals}, {0: lax.ppermute(integrals, 'zh', swap)})  6.55 us
    pallas_call x1, Pallas kernels, products(): pl.pallas_call(functools.partial(product_kernel, keys, ny), in_specs=[pl....  3.83 us
    unnamed x8, local copies, waits for them, and re-layouts  3.09 us
    ppermute x1, waiting for transfers between devices, body(): near, far = ({0: integrals}, {0: lax.ppermute(integrals, 'zh', swap)})  2.35 us
  transfers between devices with their start and end apart: 16, of which 5 were waited for; matrix products, arithmetic and copies ran while one was open for 0% of the time, Pallas kernels for 0%

profile of v2, /device:TPU:1, one launch (start us, length us, event | category | flops | bytes accessed | tf_op | source)
XLA Modules:
  0.0 106.9 jit_solution(10092908072155048476)
XLA Ops:
  0.0 8.8 %collective-permute-start = (bf16[192,10240]{1,0:T(8,128)(2,1)}, bf16[192,10240]{1,0:T(8,128)(2,1)S(1)}, u32[]{:S(2)}, u32[]{:S(2)}) collective-permute-start(bf16[192,10240]{1,0:T(8,128)(2,1)} %mine.1), channel_id=1, source_target_pairs={{0,16},{16,0},{1,17},{17,1},{2,18},{18,2},{3,19},{19,3},{4,20},{20... | collective-permute-start | bytes 11796488 | tf_op jit(solution)/shard_map/ppermute | solution.py:103
  8.8 1.9 %collective-permute-start.1 = (bf16[16,10240]{1,0:T(8,128)(2,1)}, bf16[16,10240]{1,0:T(8,128)(2,1)S(1)}, u32[]{:S(2)}, u32[]{:S(2)}) collective-permute-start(bf16[16,10240]{1,0:T(8,128)(2,1)} %own.1), channel_id=1, source_target_pairs={{0,224},{16,48},{32,0},{48,80},{64,32},{80,112},{96,64},{112,144},... | collective-permute-start | bytes 983048 | tf_op jit(solution)/shard_map/ppermute | solution.py:97
  10.7 6.5 %collective-permute-start.6 = (bf16[16,10240]{1,0:T(8,128)(2,1)}, bf16[16,10240]{1,0:T(8,128)(2,1)S(1)}, u32[]{:S(2)}, u32[]{:S(2)}) collective-permute-start(bf16[16,10240]{1,0:T(8,128)(2,1)} %own.1), channel_id=1, source_target_pairs={{0,256},{256,0},{1,257},{257,1},{2,258},{258,2},{3,259},{259,3},{4... | collective-permute-start | bytes 983048 | tf_op jit(solution)/shard_map/ppermute | solution.py:99
  17.3 3.8 %collective-permute-start.2 = (bf16[16,10240]{1,0:T(8,128)(2,1)}, bf16[16,10240]{1,0:T(8,128)(2,1)S(1)}, u32[]{:S(2)}, u32[]{:S(2)}) collective-permute-start(bf16[16,10240]{1,0:T(8,128)(2,1)} %own.1), channel_id=1, source_target_pairs={{0,32},{16,240},{32,64},{48,16},{64,96},{80,48},{96,128},{112,80},... | collective-permute-start | bytes 983048 | tf_op jit(solution)/shard_map/ppermute | solution.py:97
  21.1 0.0 collective-permute-done.1.refs_1_
  21.1 1.9 %collective-permute-start.3 = (bf16[16,10240]{1,0:T(8,128)(2,1)S(1)}, bf16[16,10240]{1,0:T(8,128)(2,1)S(1)}, u32[]{:S(2)}, u32[]{:S(2)}) collective-permute-start(bf16[16,10240]{1,0:T(8,128)(2,1)S(1)} %collective-permute-done.1.refs_1_), channel_id=1, source_target_pairs={{0,224},{16,48},{32,0},{48,80},{64,32},{80,112},{96,64},{112,144},... | collective-permute-start | bytes 983048 | tf_op jit(solution)/shard_map/ppermute | solution.py:97
  23.0 2.3 %collective-permute-done.6.refs_8_ = bf16[16,10240]{1,0:T(8,128)(2,1)S(1)} collective-permute-done((bf16[16,10240]{1,0:T(8,128)(2,1)}, bf16[16,10240]{1,0:T(8,128)(2,1)S(1)}, u32[]{:S(2)}, u32[]{:S(2)}) %collective-permute-start.6) | collective-permute-done | bytes 327712 | tf_op jit(solution)/shard_map/ppermute | solution.py:99
  25.4 3.0 %collective-permute-start.7 = (bf16[16,10240]{1,0:T(8,128)(2,1)S(1)}, bf16[16,10240]{1,0:T(8,128)(2,1)S(1)}, u32[]{:S(2)}, u32[]{:S(2)}) collective-permute-start(bf16[16,10240]{1,0:T(8,128)(2,1)S(1)} %collective-permute-done.6.refs_8_), channel_id=1, source_target_pairs={{0,224},{16,48},{32,0},{48,80},{64,32},{80,112},{96,64},{112,144},... | collective-permute-start | bytes 983048 | tf_op jit(solution)/shard_map/ppermute | solution.py:97
  28.4 5.9 %collective-permute-start.11 = (bf16[16,10240]{1,0:T(8,128)(2,1)S(1)}, bf16[16,10240]{1,0:T(8,128)(2,1)S(1)}, u32[]{:S(2)}, u32[]{:S(2)}) collective-permute-start(bf16[16,10240]{1,0:T(8,128)(2,1)S(1)} %collective-permute-done.6.refs_8_), channel_id=1, source_target_pairs={{0,32},{16,240},{32,64},{48,16},{64,96},{80,48},{96,128},{112,80},... | collective-permute-start | bytes 983048 | tf_op jit(solution)/shard_map/ppermute | solution.py:97
  34.3 3.4 %collective-permute-start.4 = (bf16[16,10240]{1,0:T(8,128)(2,1)S(1)}, bf16[16,10240]{1,0:T(8,128)(2,1)S(1)}, u32[]{:S(2)}, u32[]{:S(2)}) collective-permute-start(bf16[16,10240]{1,0:T(8,128)(2,1)S(1)} %collective-permute-done.2.refs_2_), channel_id=1, source_target_pairs={{0,32},{16,240},{32,64},{48,16},{64,96},{80,48},{96,128},{112,80},... | collective-permute-start | bytes 983048 | tf_op jit(solution)/shard_map/ppermute | solution.py:97
  37.7 0.0 collective-permute-done.3.refs_3_
  37.7 4.3 %collective-permute-start.5 = (bf16[16,10240]{1,0:T(8,128)(2,1)S(1)}, bf16[16,10240]{1,0:T(8,128)(2,1)S(1)}, u32[]{:S(2)}, u32[]{:S(2)}) collective-permute-start(bf16[16,10240]{1,0:T(8,128)(2,1)S(1)} %collective-permute-done.3.refs_3_), channel_id=1, source_target_pairs={{0,224},{16,48},{32,0},{48,80},{64,32},{80,112},{96,64},{112,144},... | collective-permute-start | bytes 983048 | tf_op jit(solution)/shard_map/ppermute | solution.py:97
  42.0 3.7 %collective-permute-start.8 = (bf16[16,10240]{1,0:T(8,128)(2,1)S(1)}, bf16[16,10240]{1,0:T(8,128)(2,1)S(1)}, u32[]{:S(2)}, u32[]{:S(2)}) collective-permute-start(bf16[16,10240]{1,0:T(8,128)(2,1)S(1)} %collective-permute-done.7.refs_9_), channel_id=1, source_target_pairs={{0,224},{16,48},{32,0},{48,80},{64,32},{80,112},{96,64},{112,144},... | collective-permute-start | bytes 983048 | tf_op jit(solution)/shard_map/ppermute | solution.py:97
  45.7 0.0 collective-permute-done.11.refs_10_
  45.7 2.8 %collective-permute-start.12 = (bf16[16,10240]{1,0:T(8,128)(2,1)S(1)}, bf16[16,10240]{1,0:T(8,128)(2,1)S(1)}, u32[]{:S(2)}, u32[]{:S(2)}) collective-permute-start(bf16[16,10240]{1,0:T(8,128)(2,1)S(1)} %collective-permute-done.11.refs_10_), channel_id=1, source_target_pairs={{0,32},{16,240},{32,64},{48,16},{64,96},{80,48},{96,128},{112,80},... | collective-permute-start | bytes 983048 | tf_op jit(solution)/shard_map/ppermute | solution.py:97
  48.5 2.1 %collective-permute-done.4.refs_4_ = bf16[16,10240]{1,0:T(8,128)(2,1)S(1)} collective-permute-done((bf16[16,10240]{1,0:T(8,128)(2,1)S(1)}, bf16[16,10240]{1,0:T(8,128)(2,1)S(1)}, u32[]{:S(2)}, u32[]{:S(2)}) %collective-permute-start.4) | collective-permute-done | bytes 327712 | tf_op jit(solution)/shard_map/ppermute | solution.py:97
  50.6 1.9 %collective-permute-start.13 = (bf16[16,10240]{1,0:T(8,128)(2,1)S(1)}, bf16[16,10240]{1,0:T(8,128)(2,1)S(1)}, u32[]{:S(2)}, u32[]{:S(2)}) collective-permute-start(bf16[16,10240]{1,0:T(8,128)(2,1)S(1)} %collective-permute-done.4.refs_4_), channel_id=1, source_target_pairs={{0,32},{16,240},{32,64},{48,16},{64,96},{80,48},{96,128},{112,80},... | collective-permute-start | bytes 983048 | tf_op jit(solution)/shard_map/ppermute | solution.py:97
  52.6 5.6 %collective-permute-start.10 = (bf16[16,10240]{1,0:T(8,128)(2,1)S(1)}, bf16[16,10240]{1,0:T(8,128)(2,1)S(1)}, u32[]{:S(2)}, u32[]{:S(2)}) collective-permute-start(bf16[16,10240]{1,0:T(8,128)(2,1)S(1)} %collective-permute-done.5.refs_5_), channel_id=1, source_target_pairs={{0,224},{16,48},{32,0},{48,80},{64,32},{80,112},{96,64},{112,144},... | collective-permute-start | bytes 983048 | tf_op jit(solution)/shard_map/ppermute | solution.py:97
  58.2 3.4 %collective-permute-start.9 = (bf16[16,10240]{1,0:T(8,128)(2,1)S(1)}, bf16[16,10240]{1,0:T(8,128)(2,1)S(1)}, u32[]{:S(2)}, u32[]{:S(2)}) collective-permute-start(bf16[16,10240]{1,0:T(8,128)(2,1)S(1)} %collective-permute-done.8.refs_11_), channel_id=1, source_target_pairs={{0,224},{16,48},{32,0},{48,80},{64,32},{80,112},{96,64},{112,144},... | collective-permute-start | bytes 983048 | tf_op jit(solution)/shard_map/ppermute | solution.py:97
  61.5 2.9 %collective-permute-done.13.refs_6_ = bf16[16,10240]{1,0:T(8,128)(2,1)S(1)} collective-permute-done((bf16[16,10240]{1,0:T(8,128)(2,1)S(1)}, bf16[16,10240]{1,0:T(8,128)(2,1)S(1)}, u32[]{:S(2)}, u32[]{:S(2)}) %collective-permute-start.13) | collective-permute-done | bytes 327712 | tf_op jit(solution)/shard_map/ppermute | solution.py:97
  64.4 1.9 %collective-permute-start.14 = (bf16[16,10240]{1,0:T(8,128)(2,1)S(1)}, bf16[16,10240]{1,0:T(8,128)(2,1)S(1)}, u32[]{:S(2)}, u32[]{:S(2)}) collective-permute-start(bf16[16,10240]{1,0:T(8,128)(2,1)S(1)} %collective-permute-done.12.refs_12_), channel_id=1, source_target_pairs={{0,32},{16,240},{32,64},{48,16},{64,96},{80,48},{96,128},{112,80},... | collective-permute-start | bytes 983048 | tf_op jit(solution)/shard_map/ppermute | solution.py:97
  66.3 0.9 collective-permute-done.9.refs_13_
  67.2 4.9 %collective-permute-start.15 = (bf16[16,10240]{1,0:T(8,128)(2,1)S(1)}, bf16[16,10240]{1,0:T(8,128)(2,1)S(1)}, u32[]{:S(2)}, u32[]{:S(2)}) collective-permute-start(bf16[16,10240]{1,0:T(8,128)(2,1)S(1)} %collective-permute-done.9.refs_13_), channel_id=1, source_target_pairs={{0,224},{16,48},{32,0},{48,80},{64,32},{80,112},{96,64},{112,144},... | collective-permute-start | bytes 983048 | tf_op jit(solution)/shard_map/ppermute | solution.py:97
  72.1 2.1 %copy-done = bf16[192,10240]{1,0:T(8,128)(2,1)S(1)} copy-done((bf16[192,10240]{1,0:T(8,128)(2,1)S(1)}, bf16[192,10240]{1,0:T(8,128)(2,1)}, u32[]{:S(2)}) %copy-start) | copy-done | bytes 3932184
  74.2 1.0 copy-done.1
  75.2 0.4 shard_map.46
  75.6 1.3 %collective-permute-done.14.refs_14_ = bf16[16,10240]{1,0:T(8,128)(2,1)S(1)} collective-permute-done((bf16[16,10240]{1,0:T(8,128)(2,1)S(1)}, bf16[16,10240]{1,0:T(8,128)(2,1)S(1)}, u32[]{:S(2)}, u32[]{:S(2)}) %collective-permute-start.14) | collective-permute-done | bytes 327712 | tf_op jit(solution)/shard_map/ppermute | solution.py:97
  76.9 0.0 copy-start.3
  76.9 3.8 %shard_map.47 = f32[32,24,128]{2,1,0:T(8,128)S(1)} custom-call(bf16[192,10240]{1,0:T(8,128)(2,1)S(1)} %get-tuple-element.12.mine, bf16[192,10240]{1,0:T(8,128)(2,1)S(1)} %collective-permute-done.other, bf16[16,10240]{1,0:T(8,128)(2,1)S(1)} %get-tuple-element.13.refs_0_, bf16[16,10240]{1,0:T(8,128)(2,1)S(1)} %collective-permute-done.1.refs_1_, ...), custom_call_target="tpu_custom_call" | custom-call | flops 2013265920 | bytes 13107200 | tf_op jit(solution)/shard_map/pallas_call | solution.py:74
  80.7 25.3 %all_to_all.5 = f32[32,24,128]{2,1,0:T(8,128)S(1)} all-to-all(f32[32,24,128]{2,1,0:T(8,128)S(1)} %shard_map.47), channel_id=1, replica_groups=mesh['zh'=2,'y'=8,'core'=2,'zl'=4,'x'=4] {'core','zl','x'}, dimensions={0} | all-to-all | bytes 786432 | tf_op jit(solution)/shard_map/all_to_all | solution.py:116
  106.1 0.1 fusion
  106.2 0.7 bitcast_divide_fusion
  (16 shorter events, 0.1 us)
Async XLA Ops:
  0.0 76.9 %collective-permute-start = (bf16[192,10240]{1,0:T(8,128)(2,1)}, bf16[192,10240]{1,0:T(8,128)(2,1)S(1)}, u32[]{:S(2)}, u32[]{:S(2)}) collective-permute-start(bf16[192,10240]{1,0:T(8,128)(2,1)} %mine.1), channel_id=1, source_target_pairs={{0,16},{16,0},{1,17},{17,1},{2,18},{18,2},{3,19},{19,3},{4,20},{20... | collective-permute-start | bytes 11796488 | tf_op jit(solution)/shard_map/ppermute | solution.py:103
  8.8 12.3 %collective-permute-start.1 = (bf16[16,10240]{1,0:T(8,128)(2,1)}, bf16[16,10240]{1,0:T(8,128)(2,1)S(1)}, u32[]{:S(2)}, u32[]{:S(2)}) collective-permute-start(bf16[16,10240]{1,0:T(8,128)(2,1)} %own.1), channel_id=1, source_target_pairs={{0,224},{16,48},{32,0},{48,80},{64,32},{80,112},{96,64},{112,144},... | collective-permute-start | bytes 983048 | tf_op jit(solution)/shard_map/ppermute | solution.py:97
  10.7 14.7 %collective-permute-start.6 = (bf16[16,10240]{1,0:T(8,128)(2,1)}, bf16[16,10240]{1,0:T(8,128)(2,1)S(1)}, u32[]{:S(2)}, u32[]{:S(2)}) collective-permute-start(bf16[16,10240]{1,0:T(8,128)(2,1)} %own.1), channel_id=1, source_target_pairs={{0,256},{256,0},{1,257},{257,1},{2,258},{258,2},{3,259},{259,3},{4... | collective-permute-start | bytes 983048 | tf_op jit(solution)/shard_map/ppermute | solution.py:99
  17.3 17.0 %collective-permute-start.2 = (bf16[16,10240]{1,0:T(8,128)(2,1)}, bf16[16,10240]{1,0:T(8,128)(2,1)S(1)}, u32[]{:S(2)}, u32[]{:S(2)}) collective-permute-start(bf16[16,10240]{1,0:T(8,128)(2,1)} %own.1), channel_id=1, source_target_pairs={{0,32},{16,240},{32,64},{48,16},{64,96},{80,48},{96,128},{112,80},... | collective-permute-start | bytes 983048 | tf_op jit(solution)/shard_map/ppermute | solution.py:97
  21.1 16.6 %collective-permute-start.3 = (bf16[16,10240]{1,0:T(8,128)(2,1)S(1)}, bf16[16,10240]{1,0:T(8,128)(2,1)S(1)}, u32[]{:S(2)}, u32[]{:S(2)}) collective-permute-start(bf16[16,10240]{1,0:T(8,128)(2,1)S(1)} %collective-permute-done.1.refs_1_), channel_id=1, source_target_pairs={{0,224},{16,48},{32,0},{48,80},{64,32},{80,112},{96,64},{112,144},... | collective-permute-start | bytes 983048 | tf_op jit(solution)/shard_map/ppermute | solution.py:97
  25.4 16.6 %collective-permute-start.7 = (bf16[16,10240]{1,0:T(8,128)(2,1)S(1)}, bf16[16,10240]{1,0:T(8,128)(2,1)S(1)}, u32[]{:S(2)}, u32[]{:S(2)}) collective-permute-start(bf16[16,10240]{1,0:T(8,128)(2,1)S(1)} %collective-permute-done.6.refs_8_), channel_id=1, source_target_pairs={{0,224},{16,48},{32,0},{48,80},{64,32},{80,112},{96,64},{112,144},... | collective-permute-start | bytes 983048 | tf_op jit(solution)/shard_map/ppermute | solution.py:97
  28.4 17.3 %collective-permute-start.11 = (bf16[16,10240]{1,0:T(8,128)(2,1)S(1)}, bf16[16,10240]{1,0:T(8,128)(2,1)S(1)}, u32[]{:S(2)}, u32[]{:S(2)}) collective-permute-start(bf16[16,10240]{1,0:T(8,128)(2,1)S(1)} %collective-permute-done.6.refs_8_), channel_id=1, source_target_pairs={{0,32},{16,240},{32,64},{48,16},{64,96},{80,48},{96,128},{112,80},... | collective-permute-start | bytes 983048 | tf_op jit(solution)/shard_map/ppermute | solution.py:97
  34.3 16.3 %collective-permute-start.4 = (bf16[16,10240]{1,0:T(8,128)(2,1)S(1)}, bf16[16,10240]{1,0:T(8,128)(2,1)S(1)}, u32[]{:S(2)}, u32[]{:S(2)}) collective-permute-start(bf16[16,10240]{1,0:T(8,128)(2,1)S(1)} %collective-permute-done.2.refs_2_), channel_id=1, source_target_pairs={{0,32},{16,240},{32,64},{48,16},{64,96},{80,48},{96,128},{112,80},... | collective-permute-start | bytes 983048 | tf_op jit(solution)/shard_map/ppermute | solution.py:97
  37.7 14.9 %collective-permute-start.5 = (bf16[16,10240]{1,0:T(8,128)(2,1)S(1)}, bf16[16,10240]{1,0:T(8,128)(2,1)S(1)}, u32[]{:S(2)}, u32[]{:S(2)}) collective-permute-start(bf16[16,10240]{1,0:T(8,128)(2,1)S(1)} %collective-permute-done.3.refs_3_), channel_id=1, source_target_pairs={{0,224},{16,48},{32,0},{48,80},{64,32},{80,112},{96,64},{112,144},... | collective-permute-start | bytes 983048 | tf_op jit(solution)/shard_map/ppermute | solution.py:97
  42.0 16.1 %collective-permute-start.8 = (bf16[16,10240]{1,0:T(8,128)(2,1)S(1)}, bf16[16,10240]{1,0:T(8,128)(2,1)S(1)}, u32[]{:S(2)}, u32[]{:S(2)}) collective-permute-start(bf16[16,10240]{1,0:T(8,128)(2,1)S(1)} %collective-permute-done.7.refs_9_), channel_id=1, source_target_pairs={{0,224},{16,48},{32,0},{48,80},{64,32},{80,112},{96,64},{112,144},... | collective-permute-start | bytes 983048 | tf_op jit(solution)/shard_map/ppermute | solution.py:97
  45.7 15.8 %collective-permute-start.12 = (bf16[16,10240]{1,0:T(8,128)(2,1)S(1)}, bf16[16,10240]{1,0:T(8,128)(2,1)S(1)}, u32[]{:S(2)}, u32[]{:S(2)}) collective-permute-start(bf16[16,10240]{1,0:T(8,128)(2,1)S(1)} %collective-permute-done.11.refs_10_), channel_id=1, source_target_pairs={{0,32},{16,240},{32,64},{48,16},{64,96},{80,48},{96,128},{112,80},... | collective-permute-start | bytes 983048 | tf_op jit(solution)/shard_map/ppermute | solution.py:97
  50.6 13.8 %collective-permute-start.13 = (bf16[16,10240]{1,0:T(8,128)(2,1)S(1)}, bf16[16,10240]{1,0:T(8,128)(2,1)S(1)}, u32[]{:S(2)}, u32[]{:S(2)}) collective-permute-start(bf16[16,10240]{1,0:T(8,128)(2,1)S(1)} %collective-permute-done.4.refs_4_), channel_id=1, source_target_pairs={{0,32},{16,240},{32,64},{48,16},{64,96},{80,48},{96,128},{112,80},... | collective-permute-start | bytes 983048 | tf_op jit(solution)/shard_map/ppermute | solution.py:97
  52.6 13.8 %collective-permute-start.10 = (bf16[16,10240]{1,0:T(8,128)(2,1)S(1)}, bf16[16,10240]{1,0:T(8,128)(2,1)S(1)}, u32[]{:S(2)}, u32[]{:S(2)}) collective-permute-start(bf16[16,10240]{1,0:T(8,128)(2,1)S(1)} %collective-permute-done.5.refs_5_), channel_id=1, source_target_pairs={{0,224},{16,48},{32,0},{48,80},{64,32},{80,112},{96,64},{112,144},... | collective-permute-start | bytes 983048 | tf_op jit(solution)/shard_map/ppermute | solution.py:97
  58.2 9.0 %collective-permute-start.9 = (bf16[16,10240]{1,0:T(8,128)(2,1)S(1)}, bf16[16,10240]{1,0:T(8,128)(2,1)S(1)}, u32[]{:S(2)}, u32[]{:S(2)}) collective-permute-start(bf16[16,10240]{1,0:T(8,128)(2,1)S(1)} %collective-permute-done.8.refs_11_), channel_id=1, source_target_pairs={{0,224},{16,48},{32,0},{48,80},{64,32},{80,112},{96,64},{112,144},... | collective-permute-start | bytes 983048 | tf_op jit(solution)/shard_map/ppermute | solution.py:97
  64.4 12.5 %collective-permute-start.14 = (bf16[16,10240]{1,0:T(8,128)(2,1)S(1)}, bf16[16,10240]{1,0:T(8,128)(2,1)S(1)}, u32[]{:S(2)}, u32[]{:S(2)}) collective-permute-start(bf16[16,10240]{1,0:T(8,128)(2,1)S(1)} %collective-permute-done.12.refs_12_), channel_id=1, source_target_pairs={{0,32},{16,240},{32,64},{48,16},{64,96},{80,48},{96,128},{112,80},... | collective-permute-start | bytes 983048 | tf_op jit(solution)/shard_map/ppermute | solution.py:97
  67.2 9.7 %collective-permute-start.15 = (bf16[16,10240]{1,0:T(8,128)(2,1)S(1)}, bf16[16,10240]{1,0:T(8,128)(2,1)S(1)}, u32[]{:S(2)}, u32[]{:S(2)}) collective-permute-start(bf16[16,10240]{1,0:T(8,128)(2,1)S(1)} %collective-permute-done.9.refs_13_), channel_id=1, source_target_pairs={{0,224},{16,48},{32,0},{48,80},{64,32},{80,112},{96,64},{112,144},... | collective-permute-start | bytes 983048 | tf_op jit(solution)/shard_map/ppermute | solution.py:97
  72.1 2.1 %copy-start = (bf16[192,10240]{1,0:T(8,128)(2,1)S(1)}, bf16[192,10240]{1,0:T(8,128)(2,1)}, u32[]{:S(2)}) copy-start(bf16[192,10240]{1,0:T(8,128)(2,1)} %mine.1) | copy-start | bytes 11796484
  74.2 1.0 copy-start.1
  76.9 29.3 %copy-start.2 = (f32[192]{0:T(256)S(1)}, f32[192]{0:T(256)}, u32[]{:S(2)}) copy-start(f32[192]{0:T(256)} %param.6) | copy-start | bytes 2308
  76.9 29.3 %copy-start.3 = (f32[32]{0:T(128)S(1)}, f32[32]{0:T(128)}, u32[]{:S(2)}) copy-start(f32[32]{0:T(128)} %param.7) | copy-start | bytes 388

commit v3 on v2

--- a/solution.py
+++ b/solution.py
@@ -12,7 +12,7 @@
 LANES = 128
 
 
-def product_kernel(keys, ny, mine, other, *refs):
+def product_kernel(keys, ny, mark, mine, other, *refs):
     n = len(keys)
     blocks, out, acc = refs[:n], refs[n], refs[n + 1]
     rows, depth = mine.shape
@@ -67,13 +67,28 @@
     )(mine, own)
 
 
-def products(keys, ny, mine, other, blocks):
+def mark_kernel(block, out):
+    out[...] = jnp.zeros_like(out)
+
+
+def mark_after(block):
+    return pl.pallas_call(
+        mark_kernel,
+        in_specs=[pl.BlockSpec(memory_space=pl.ANY)],
+        out_specs=pl.BlockSpec(memory_space=pltpu.VMEM),
+        out_shape=jax.ShapeDtypeStruct((8, LANES), jnp.int32),
+        compiler_params=pltpu.CompilerParams(vmem_limit_bytes=1024 * 1024),
+        cost_estimate=pl.CostEstimate(flops=46_000_000_000, bytes_accessed=0, transcendentals=0),
+    )(block)
+
+
+def products(keys, ny, mark, mine, other, blocks):
     n = len(blocks)
     rows, depth = mine.shape
     height = blocks[0].shape[0]
     return pl.pallas_call(
         functools.partial(product_kernel, keys, ny),
-        in_specs=[pl.BlockSpec(memory_space=pltpu.VMEM)] * (2 + n),
+        in_specs=[pl.BlockSpec(memory_space=pl.ANY)] + [pl.BlockSpec(memory_space=pltpu.VMEM)] * (2 + n),
         out_specs=pl.BlockSpec(memory_space=pltpu.VMEM),
         out_shape=jax.ShapeDtypeStruct((2 * n, height * rows // LANES, LANES), jnp.float32),
         scratch_shapes=[pltpu.VMEM((2, rows, n * height), jnp.float32)],
@@ -83,7 +98,7 @@
             bytes_accessed=2 * (2 * rows + n * height) * depth,
             transcendentals=0,
         ),
-    )(mine, other, *blocks)
+    )(mark, mine, other, *blocks)
 
 
 def body(sizes, amplitudes, integrals, occ_pair, vir_pair):
@@ -97,22 +112,26 @@
         return lax.ppermute(block, ("y", "core"), pairs)
 
     near, far = {0: integrals}, {0: lax.ppermute(integrals, "zh", swap)}
-    for s in (1, 2, 3):
-        near[s], near[-s] = hop(near[s - 1], 1), hop(near[1 - s], -1)
+    near[1], near[-1] = hop(near[0], 1), hop(near[0], -1)
+    near[2], near[-2] = hop(near[1], 1), hop(near[-1], -1)
+    other = lax.ppermute(amplitudes, "core", swap)
+    far[0], mark = tie((far[0], mark_after(far[0])))
+    far[1] = hop(far[0], 1)
+    last, near[2] = tie((far[0], near[2]))
+    far[-1] = hop(last, -1)
+    near[3], near[-3] = hop(near[2], 1), hop(near[-2], -1)
+    last, other = tie((far[1], other))
+    far[2] = hop(last, 1)
+    far[-2] = hop(far[-1], -1)
     near[4] = hop(near[3], 1)
-    other = lax.ppermute(amplitudes, "core", swap)
-    for s in (1, 2):
-        far[s], far[-s] = hop(far[s - 1], 1), hop(far[1 - s], -1)
-    far[3] = hop(far[2], 1)
-    last, near[-3] = tie((far[-2], near[-3]))
-    far[-3] = hop(last, -1)
-    last, near[4], near[-3] = tie((far[3], near[4], near[-3]))
-    far[4] = hop(last, 1)
+    last, near[-2] = tie((far[2], near[-2]))
+    far[3], far[-3] = hop(last, 1), hop(far[-2], -1)
+    far[4] = hop(far[3], 1)
 
     held = {(p, s): block for p, plane in enumerate((near, far)) for s, block in plane.items()}
     mine, held[0, 0] = fetch(amplitudes, integrals)
     keys = list(held)
-    sent = products(keys, ny, mine, other, [held[k] for k in keys])
+    sent = products(keys, ny, mark, mine, other, [held[k] for k in keys])
     got = lax.all_to_all(sent, ("core", "zl", "x"), 0, 0, tiled=True)
     total = got.reshape(2, 2 * ny, -1, LANES).sum(axis=1)
     left, rest = total[:, :height], total[:, height:]

time: 108 us -> 104 us (0.963)
  local copies, waits for them, and re-layouts: 3.16 us -> 0.09 us
  waiting for transfers between devices: 9.47 us -> 7.55 us
  starting transfers between devices: 63.7 us -> 65 us
    ppermute x1, starting transfers between devices: 8.77 us -> 3.14 us  [body(): other = lax.ppermute(amplitudes, 'core', swap)]
    ppermute x1, starting transfers between devices: 6.55 us -> 10.6 us  [body(): near, far = ({0: integrals}, {0: lax.ppermute(integrals, 'zh', swap)})]
    unnamed x8, local copies, waits for them, and re-layouts: 3.09 us -> 0.01 us
    ppermute x14, starting transfers between devices: 48.4 us -> 51.2 us  [hop(): return lax.ppermute(block, ('y', 'core'), pairs)]
    ppermute x1, waiting for transfers between devices: 2.35 us -> 0.01 us  [body(): near, far = ({0: integrals}, {0: lax.ppermute(integrals, 'zh', swap)})]
  transfers between devices with their start and end apart: 16 -> 16, of which waited for: 5 -> 3; matrix products, arithmetic and copies ran while one was open for 0% -> 0% of each run, Pallas kernels for 0% -> 0%
where the time goes in v3:
time: 104 us; the launch traced here: 103 us
  starting transfers between devices  65 us (62%)
  blocking collectives  25.1 us (24%)
  waiting for transfers between devices  7.55 us (7%)
  Pallas kernels  4.16 us (4%)
    ppermute x14, starting transfers between devices, hop(): return lax.ppermute(block, ('y', 'core'), pairs)  51.2 us
    all_to_all x1, blocking collectives, body(): got = lax.all_to_all(sent, ('core', 'zl', 'x'), 0, 0, tiled=True)  25.1 us
    ppermute x1, starting transfers between devices, body(): near, far = ({0: integrals}, {0: lax.ppermute(integrals, 'zh', swap)})  10.6 us
    ppermute x14, waiting for transfers between devices, hop(): return lax.ppermute(block, ('y', 'core'), pairs)  7.55 us
    pallas_call x1, Pallas kernels, products(): pl.pallas_call(functools.partial(product_kernel, keys, ny), in_specs=[pl....  3.78 us
    ppermute x1, starting transfers between devices, body(): other = lax.ppermute(amplitudes, 'core', swap)  3.14 us
  transfers between devices with their start and end apart: 16, of which 3 were waited for; matrix products, arithmetic and copies ran while one was open for 0% of the time, Pallas kernels for 0%

profile of v3, /device:TPU:1, one launch (start us, length us, event | category | flops | bytes accessed | tf_op | source)
XLA Modules:
  0.0 103.0 jit_solution(6899786904047714351)
XLA Ops:
  0.0 4.3 %collective-permute-start.3 = (bf16[16,10240]{1,0:T(8,128)(2,1)}, bf16[16,10240]{1,0:T(8,128)(2,1)S(1)}, u32[]{:S(2)}, u32[]{:S(2)}) collective-permute-start(bf16[16,10240]{1,0:T(8,128)(2,1)} %own.1), channel_id=1, source_target_pairs={{0,224},{16,48},{32,0},{48,80},{64,32},{80,112},{96,64},{112,144},... | collective-permute-start | bytes 983048 | tf_op jit(solution)/shard_map/ppermute | solution.py:112
  4.3 10.6 %collective-permute-start = (bf16[16,10240]{1,0:T(8,128)(2,1)}, bf16[16,10240]{1,0:T(8,128)(2,1)S(1)}, u32[]{:S(2)}, u32[]{:S(2)}) collective-permute-start(bf16[16,10240]{1,0:T(8,128)(2,1)} %own.1), channel_id=1, source_target_pairs={{0,256},{256,0},{1,257},{257,1},{2,258},{258,2},{3,259},{259,3},{4... | collective-permute-start | bytes 983048 | tf_op jit(solution)/shard_map/ppermute | solution.py:114
  14.9 3.8 %collective-permute-start.4 = (bf16[16,10240]{1,0:T(8,128)(2,1)}, bf16[16,10240]{1,0:T(8,128)(2,1)S(1)}, u32[]{:S(2)}, u32[]{:S(2)}) collective-permute-start(bf16[16,10240]{1,0:T(8,128)(2,1)} %own.1), channel_id=1, source_target_pairs={{0,32},{16,240},{32,64},{48,16},{64,96},{80,48},{96,128},{112,80},... | collective-permute-start | bytes 983048 | tf_op jit(solution)/shard_map/ppermute | solution.py:112
  18.8 3.1 %collective-permute-start.2 = (bf16[192,10240]{1,0:T(8,128)(2,1)}, bf16[192,10240]{1,0:T(8,128)(2,1)S(1)}, u32[]{:S(2)}, u32[]{:S(2)}) collective-permute-start(bf16[192,10240]{1,0:T(8,128)(2,1)} %mine.1), channel_id=1, source_target_pairs={{0,16},{16,0},{1,17},{17,1},{2,18},{18,2},{3,19},{19,3},{4,20},{20... | collective-permute-start | bytes 11796488 | tf_op jit(solution)/shard_map/ppermute | solution.py:117
  21.9 1.9 %collective-permute-start.5 = (bf16[16,10240]{1,0:T(8,128)(2,1)S(1)}, bf16[16,10240]{1,0:T(8,128)(2,1)S(1)}, u32[]{:S(2)}, u32[]{:S(2)}) collective-permute-start(bf16[16,10240]{1,0:T(8,128)(2,1)S(1)} %collective-permute-done.3.refs_1_), channel_id=1, source_target_pairs={{0,224},{16,48},{32,0},{48,80},{64,32},{80,112},{96,64},{112,144},... | collective-permute-start | bytes 983048 | tf_op jit(solution)/shard_map/ppermute | solution.py:112
  23.9 0.0 collective-permute-done.block.refs_8_
  23.9 3.0 %collective-permute-start.1 = (bf16[16,10240]{1,0:T(8,128)(2,1)S(1)}, bf16[16,10240]{1,0:T(8,128)(2,1)S(1)}, u32[]{:S(2)}, u32[]{:S(2)}) collective-permute-start(bf16[16,10240]{1,0:T(8,128)(2,1)S(1)} %collective-permute-done.block.refs_8_), channel_id=1, source_target_pairs={{0,224},{16,48},{32,0},{48,80},{64,32},{80,112},{96,64},{112,144},... | collective-permute-start | bytes 983048 | tf_op jit(solution)/shard_map/ppermute | solution.py:112
  26.9 0.0 collective-permute-done.4.refs_2_
  26.9 3.7 %collective-permute-start.7 = (bf16[16,10240]{1,0:T(8,128)(2,1)S(1)}, bf16[16,10240]{1,0:T(8,128)(2,1)S(1)}, u32[]{:S(2)}, u32[]{:S(2)}) collective-permute-start(bf16[16,10240]{1,0:T(8,128)(2,1)S(1)} %collective-permute-done.4.refs_2_), channel_id=1, source_target_pairs={{0,32},{16,240},{32,64},{48,16},{64,96},{80,48},{96,128},{112,80},... | collective-permute-start | bytes 983048 | tf_op jit(solution)/shard_map/ppermute | solution.py:112
  30.7 0.6 collective-permute-done.5.refs_3_
  31.3 3.6 %collective-permute-start.11 = (bf16[16,10240]{1,0:T(8,128)(2,1)S(1)}, bf16[16,10240]{1,0:T(8,128)(2,1)S(1)}, u32[]{:S(2)}, u32[]{:S(2)}) collective-permute-start(bf16[16,10240]{1,0:T(8,128)(2,1)S(1)} %collective-permute-done.block.refs_8_), channel_id=1, source_target_pairs={{0,32},{16,240},{32,64},{48,16},{64,96},{80,48},{96,128},{112,80},... | collective-permute-start | bytes 983048 | tf_op jit(solution)/shard_map/ppermute | solution.py:112
  34.9 0.0 collective-permute-done.1.refs_9_
  34.9 0.0 collective-permute-done.2.other
  34.9 1.9 %collective-permute-start.6 = (bf16[16,10240]{1,0:T(8,128)(2,1)S(1)}, bf16[16,10240]{1,0:T(8,128)(2,1)S(1)}, u32[]{:S(2)}, u32[]{:S(2)}) collective-permute-start(bf16[16,10240]{1,0:T(8,128)(2,1)S(1)} %collective-permute-done.1.refs_9_), channel_id=1, source_target_pairs={{0,224},{16,48},{32,0},{48,80},{64,32},{80,112},{96,64},{112,144},... | collective-permute-start | bytes 983048 | tf_op jit(solution)/shard_map/ppermute | solution.py:112
  36.8 8.5 %collective-permute-start.8 = (bf16[16,10240]{1,0:T(8,128)(2,1)S(1)}, bf16[16,10240]{1,0:T(8,128)(2,1)S(1)}, u32[]{:S(2)}, u32[]{:S(2)}) collective-permute-start(bf16[16,10240]{1,0:T(8,128)(2,1)S(1)} %collective-permute-done.5.refs_3_), channel_id=1, source_target_pairs={{0,224},{16,48},{32,0},{48,80},{64,32},{80,112},{96,64},{112,144},... | collective-permute-start | bytes 983048 | tf_op jit(solution)/shard_map/ppermute | solution.py:112
  45.3 0.0 collective-permute-done.11.refs_10_
  45.3 1.9 %collective-permute-start.12 = (bf16[16,10240]{1,0:T(8,128)(2,1)S(1)}, bf16[16,10240]{1,0:T(8,128)(2,1)S(1)}, u32[]{:S(2)}, u32[]{:S(2)}) collective-permute-start(bf16[16,10240]{1,0:T(8,128)(2,1)S(1)} %collective-permute-done.11.refs_10_), channel_id=1, source_target_pairs={{0,32},{16,240},{32,64},{48,16},{64,96},{80,48},{96,128},{112,80},... | collective-permute-start | bytes 983048 | tf_op jit(solution)/shard_map/ppermute | solution.py:112
  47.3 0.0 collective-permute-done.7.refs_4_
  47.3 5.0 %collective-permute-start.13 = (bf16[16,10240]{1,0:T(8,128)(2,1)S(1)}, bf16[16,10240]{1,0:T(8,128)(2,1)S(1)}, u32[]{:S(2)}, u32[]{:S(2)}) collective-permute-start(bf16[16,10240]{1,0:T(8,128)(2,1)S(1)} %collective-permute-done.6.refs_11_), channel_id=1, source_target_pairs={{0,224},{16,48},{32,0},{48,80},{64,32},{80,112},{96,64},{112,144},... | collective-permute-start | bytes 983048 | tf_op jit(solution)/shard_map/ppermute | solution.py:112
  52.3 1.9 %collective-permute-start.9 = (bf16[16,10240]{1,0:T(8,128)(2,1)S(1)}, bf16[16,10240]{1,0:T(8,128)(2,1)S(1)}, u32[]{:S(2)}, u32[]{:S(2)}) collective-permute-start(bf16[16,10240]{1,0:T(8,128)(2,1)S(1)} %collective-permute-done.7.refs_4_), channel_id=1, source_target_pairs={{0,32},{16,240},{32,64},{48,16},{64,96},{80,48},{96,128},{112,80},... | collective-permute-start | bytes 983048 | tf_op jit(solution)/shard_map/ppermute | solution.py:112
  54.2 0.0 collective-permute-done.8.refs_5_
  54.2 5.3 %collective-permute-start.10 = (bf16[16,10240]{1,0:T(8,128)(2,1)S(1)}, bf16[16,10240]{1,0:T(8,128)(2,1)S(1)}, u32[]{:S(2)}, u32[]{:S(2)}) collective-permute-start(bf16[16,10240]{1,0:T(8,128)(2,1)S(1)} %collective-permute-done.8.refs_5_), channel_id=1, source_target_pairs={{0,224},{16,48},{32,0},{48,80},{64,32},{80,112},{96,64},{112,144},... | collective-permute-start | bytes 983048 | tf_op jit(solution)/shard_map/ppermute | solution.py:112
  59.6 1.9 %collective-permute-start.14 = (bf16[16,10240]{1,0:T(8,128)(2,1)S(1)}, bf16[16,10240]{1,0:T(8,128)(2,1)S(1)}, u32[]{:S(2)}, u32[]{:S(2)}) collective-permute-start(bf16[16,10240]{1,0:T(8,128)(2,1)S(1)} %collective-permute-done.12.refs_12_), channel_id=1, source_target_pairs={{0,32},{16,240},{32,64},{48,16},{64,96},{80,48},{96,128},{112,80},... | collective-permute-start | bytes 983048 | tf_op jit(solution)/shard_map/ppermute | solution.py:112
  61.5 0.0 collective-permute-done.13.refs_13_
  61.5 4.3 %collective-permute-start.15 = (bf16[16,10240]{1,0:T(8,128)(2,1)S(1)}, bf16[16,10240]{1,0:T(8,128)(2,1)S(1)}, u32[]{:S(2)}, u32[]{:S(2)}) collective-permute-start(bf16[16,10240]{1,0:T(8,128)(2,1)S(1)} %collective-permute-done.13.refs_13_), channel_id=1, source_target_pairs={{0,224},{16,48},{32,0},{48,80},{64,32},{80,112},{96,64},{112,144},... | collective-permute-start | bytes 983048 | tf_op jit(solution)/shard_map/ppermute | solution.py:112
  65.9 0.4 shard_map.47
  66.3 5.2 %collective-permute-done.14.refs_14_ = bf16[16,10240]{1,0:T(8,128)(2,1)S(1)} collective-permute-done((bf16[16,10240]{1,0:T(8,128)(2,1)S(1)}, bf16[16,10240]{1,0:T(8,128)(2,1)S(1)}, u32[]{:S(2)}, u32[]{:S(2)}) %collective-permute-start.14) | collective-permute-done | bytes 327712 | tf_op jit(solution)/shard_map/ppermute | solution.py:112
  71.6 1.7 %collective-permute-done.15.refs_15_ = bf16[16,10240]{1,0:T(8,128)(2,1)S(1)} collective-permute-done((bf16[16,10240]{1,0:T(8,128)(2,1)S(1)}, bf16[16,10240]{1,0:T(8,128)(2,1)S(1)}, u32[]{:S(2)}, u32[]{:S(2)}) %collective-permute-start.15) | collective-permute-done | bytes 327712 | tf_op jit(solution)/shard_map/ppermute | solution.py:112
  73.2 3.8 %shard_map.48 = f32[32,24,128]{2,1,0:T(8,128)S(1)} custom-call(s32[8,128]{1,0:T(8,128)S(1)} %shard_map.46.mark, bf16[192,10240]{1,0:T(8,128)(2,1)S(1)} %get-tuple-element.16.mine, bf16[192,10240]{1,0:T(8,128)(2,1)S(1)} %collective-permute-done.2.other, bf16[16,10240]{1,0:T(8,128)(2,1)S(1)} %get-tuple-element.19.refs_0_, ...), custom_call_target="tpu_custom_call" | custom-call | flops 2013265920 | bytes 13107200 | tf_op jit(solution)/shard_map/pallas_call | solution.py:89
  77.0 25.1 %all_to_all.5 = f32[32,24,128]{2,1,0:T(8,128)S(1)} all-to-all(f32[32,24,128]{2,1,0:T(8,128)S(1)} %shard_map.48), channel_id=1, replica_groups=mesh['zh'=2,'y'=8,'core'=2,'zl'=4,'x'=4] {'core','zl','x'}, dimensions={0} | all-to-all | bytes 786432 | tf_op jit(solution)/shard_map/all_to_all | solution.py:135
  102.2 0.1 fusion
  102.3 0.7 bitcast_divide_fusion
  (17 shorter events, 0.1 us)
Async XLA Ops:
  0.0 65.9 %copy-start.1 = (bf16[16,10240]{1,0:T(8,128)(2,1)S(1)}, bf16[16,10240]{1,0:T(8,128)(2,1)}, u32[]{:S(2)}) copy-start(bf16[16,10240]{1,0:T(8,128)(2,1)} %own.1) | copy-start | bytes 983044
  0.0 65.9 %copy-start = (bf16[192,10240]{1,0:T(8,128)(2,1)S(1)}, bf16[192,10240]{1,0:T(8,128)(2,1)}, u32[]{:S(2)}) copy-start(bf16[192,10240]{1,0:T(8,128)(2,1)} %mine.1) | copy-start | bytes 11796484
  0.0 21.9 %collective-permute-start.3 = (bf16[16,10240]{1,0:T(8,128)(2,1)}, bf16[16,10240]{1,0:T(8,128)(2,1)S(1)}, u32[]{:S(2)}, u32[]{:S(2)}) collective-permute-start(bf16[16,10240]{1,0:T(8,128)(2,1)} %own.1), channel_id=1, source_target_pairs={{0,224},{16,48},{32,0},{48,80},{64,32},{80,112},{96,64},{112,144},... | collective-permute-start | bytes 983048 | tf_op jit(solution)/shard_map/ppermute | solution.py:112
  4.3 19.6 %collective-permute-start = (bf16[16,10240]{1,0:T(8,128)(2,1)}, bf16[16,10240]{1,0:T(8,128)(2,1)S(1)}, u32[]{:S(2)}, u32[]{:S(2)}) collective-permute-start(bf16[16,10240]{1,0:T(8,128)(2,1)} %own.1), channel_id=1, source_target_pairs={{0,256},{256,0},{1,257},{257,1},{2,258},{258,2},{3,259},{259,3},{4... | collective-permute-start | bytes 983048 | tf_op jit(solution)/shard_map/ppermute | solution.py:114
  14.9 12.0 %collective-permute-start.4 = (bf16[16,10240]{1,0:T(8,128)(2,1)}, bf16[16,10240]{1,0:T(8,128)(2,1)S(1)}, u32[]{:S(2)}, u32[]{:S(2)}) collective-permute-start(bf16[16,10240]{1,0:T(8,128)(2,1)} %own.1), channel_id=1, source_target_pairs={{0,32},{16,240},{32,64},{48,16},{64,96},{80,48},{96,128},{112,80},... | collective-permute-start | bytes 983048 | tf_op jit(solution)/shard_map/ppermute | solution.py:112
  18.8 16.1 %collective-permute-start.2 = (bf16[192,10240]{1,0:T(8,128)(2,1)}, bf16[192,10240]{1,0:T(8,128)(2,1)S(1)}, u32[]{:S(2)}, u32[]{:S(2)}) collective-permute-start(bf16[192,10240]{1,0:T(8,128)(2,1)} %mine.1), channel_id=1, source_target_pairs={{0,16},{16,0},{1,17},{17,1},{2,18},{18,2},{3,19},{19,3},{4,20},{20... | collective-permute-start | bytes 11796488 | tf_op jit(solution)/shard_map/ppermute | solution.py:117
  21.9 9.4 %collective-permute-start.5 = (bf16[16,10240]{1,0:T(8,128)(2,1)S(1)}, bf16[16,10240]{1,0:T(8,128)(2,1)S(1)}, u32[]{:S(2)}, u32[]{:S(2)}) collective-permute-start(bf16[16,10240]{1,0:T(8,128)(2,1)S(1)} %collective-permute-done.3.refs_1_), channel_id=1, source_target_pairs={{0,224},{16,48},{32,0},{48,80},{64,32},{80,112},{96,64},{112,144},... | collective-permute-start | bytes 983048 | tf_op jit(solution)/shard_map/ppermute | solution.py:112
  23.9 11.0 %collective-permute-start.1 = (bf16[16,10240]{1,0:T(8,128)(2,1)S(1)}, bf16[16,10240]{1,0:T(8,128)(2,1)S(1)}, u32[]{:S(2)}, u32[]{:S(2)}) collective-permute-start(bf16[16,10240]{1,0:T(8,128)(2,1)S(1)} %collective-permute-done.block.refs_8_), channel_id=1, source_target_pairs={{0,224},{16,48},{32,0},{48,80},{64,32},{80,112},{96,64},{112,144},... | collective-permute-start | bytes 983048 | tf_op jit(solution)/shard_map/ppermute | solution.py:112
  26.9 20.3 %collective-permute-start.7 = (bf16[16,10240]{1,0:T(8,128)(2,1)S(1)}, bf16[16,10240]{1,0:T(8,128)(2,1)S(1)}, u32[]{:S(2)}, u32[]{:S(2)}) collective-permute-start(bf16[16,10240]{1,0:T(8,128)(2,1)S(1)} %collective-permute-done.4.refs_2_), channel_id=1, source_target_pairs={{0,32},{16,240},{32,64},{48,16},{64,96},{80,48},{96,128},{112,80},... | collective-permute-start | bytes 983048 | tf_op jit(solution)/shard_map/ppermute | solution.py:112
  31.3 14.0 %collective-permute-start.11 = (bf16[16,10240]{1,0:T(8,128)(2,1)S(1)}, bf16[16,10240]{1,0:T(8,128)(2,1)S(1)}, u32[]{:S(2)}, u32[]{:S(2)}) collective-permute-start(bf16[16,10240]{1,0:T(8,128)(2,1)S(1)} %collective-permute-done.block.refs_8_), channel_id=1, source_target_pairs={{0,32},{16,240},{32,64},{48,16},{64,96},{80,48},{96,128},{112,80},... | collective-permute-start | bytes 983048 | tf_op jit(solution)/shard_map/ppermute | solution.py:112
  34.9 12.4 %collective-permute-start.6 = (bf16[16,10240]{1,0:T(8,128)(2,1)S(1)}, bf16[16,10240]{1,0:T(8,128)(2,1)S(1)}, u32[]{:S(2)}, u32[]{:S(2)}) collective-permute-start(bf16[16,10240]{1,0:T(8,128)(2,1)S(1)} %collective-permute-done.1.refs_9_), channel_id=1, source_target_pairs={{0,224},{16,48},{32,0},{48,80},{64,32},{80,112},{96,64},{112,144},... | collective-permute-start | bytes 983048 | tf_op jit(solution)/shard_map/ppermute | solution.py:112
  36.8 17.4 %collective-permute-start.8 = (bf16[16,10240]{1,0:T(8,128)(2,1)S(1)}, bf16[16,10240]{1,0:T(8,128)(2,1)S(1)}, u32[]{:S(2)}, u32[]{:S(2)}) collective-permute-start(bf16[16,10240]{1,0:T(8,128)(2,1)S(1)} %collective-permute-done.5.refs_3_), channel_id=1, source_target_pairs={{0,224},{16,48},{32,0},{48,80},{64,32},{80,112},{96,64},{112,144},... | collective-permute-start | bytes 983048 | tf_op jit(solution)/shard_map/ppermute | solution.py:112
  45.3 14.3 %collective-permute-start.12 = (bf16[16,10240]{1,0:T(8,128)(2,1)S(1)}, bf16[16,10240]{1,0:T(8,128)(2,1)S(1)}, u32[]{:S(2)}, u32[]{:S(2)}) collective-permute-start(bf16[16,10240]{1,0:T(8,128)(2,1)S(1)} %collective-permute-done.11.refs_10_), channel_id=1, source_target_pairs={{0,32},{16,240},{32,64},{48,16},{64,96},{80,48},{96,128},{112,80},... | collective-permute-start | bytes 983048 | tf_op jit(solution)/shard_map/ppermute | solution.py:112
  47.3 14.3 %collective-permute-start.13 = (bf16[16,10240]{1,0:T(8,128)(2,1)S(1)}, bf16[16,10240]{1,0:T(8,128)(2,1)S(1)}, u32[]{:S(2)}, u32[]{:S(2)}) collective-permute-start(bf16[16,10240]{1,0:T(8,128)(2,1)S(1)} %collective-permute-done.6.refs_11_), channel_id=1, source_target_pairs={{0,224},{16,48},{32,0},{48,80},{64,32},{80,112},{96,64},{112,144},... | collective-permute-start | bytes 983048 | tf_op jit(solution)/shard_map/ppermute | solution.py:112
  52.3 14.0 %collective-permute-start.9 = (bf16[16,10240]{1,0:T(8,128)(2,1)S(1)}, bf16[16,10240]{1,0:T(8,128)(2,1)S(1)}, u32[]{:S(2)}, u32[]{:S(2)}) collective-permute-start(bf16[16,10240]{1,0:T(8,128)(2,1)S(1)} %collective-permute-done.7.refs_4_), channel_id=1, source_target_pairs={{0,32},{16,240},{32,64},{48,16},{64,96},{80,48},{96,128},{112,80},... | collective-permute-start | bytes 983048 | tf_op jit(solution)/shard_map/ppermute | solution.py:112
  54.2 12.1 %collective-permute-start.10 = (bf16[16,10240]{1,0:T(8,128)(2,1)S(1)}, bf16[16,10240]{1,0:T(8,128)(2,1)S(1)}, u32[]{:S(2)}, u32[]{:S(2)}) collective-permute-start(bf16[16,10240]{1,0:T(8,128)(2,1)S(1)} %collective-permute-done.8.refs_5_), channel_id=1, source_target_pairs={{0,224},{16,48},{32,0},{48,80},{64,32},{80,112},{96,64},{112,144},... | collective-permute-start | bytes 983048 | tf_op jit(solution)/shard_map/ppermute | solution.py:112
  59.6 12.0 %collective-permute-start.14 = (bf16[16,10240]{1,0:T(8,128)(2,1)S(1)}, bf16[16,10240]{1,0:T(8,128)(2,1)S(1)}, u32[]{:S(2)}, u32[]{:S(2)}) collective-permute-start(bf16[16,10240]{1,0:T(8,128)(2,1)S(1)} %collective-permute-done.12.refs_12_), channel_id=1, source_target_pairs={{0,32},{16,240},{32,64},{48,16},{64,96},{80,48},{96,128},{112,80},... | collective-permute-start | bytes 983048 | tf_op jit(solution)/shard_map/ppermute | solution.py:112
  61.5 11.7 %collective-permute-start.15 = (bf16[16,10240]{1,0:T(8,128)(2,1)S(1)}, bf16[16,10240]{1,0:T(8,128)(2,1)S(1)}, u32[]{:S(2)}, u32[]{:S(2)}) collective-permute-start(bf16[16,10240]{1,0:T(8,128)(2,1)S(1)} %collective-permute-done.13.refs_13_), channel_id=1, source_target_pairs={{0,224},{16,48},{32,0},{48,80},{64,32},{80,112},{96,64},{112,144},... | collective-permute-start | bytes 983048 | tf_op jit(solution)/shard_map/ppermute | solution.py:112
  73.2 29.0 %copy-start.2 = (f32[192]{0:T(256)S(1)}, f32[192]{0:T(256)}, u32[]{:S(2)}) copy-start(f32[192]{0:T(256)} %param.6) | copy-start | bytes 2308
  73.2 29.0 %copy-start.3 = (f32[32]{0:T(128)S(1)}, f32[32]{0:T(128)}, u32[]{:S(2)}) copy-start(f32[32]{0:T(128)} %param.7) | copy-start | bytes 388

commit v4 on v3

--- a/solution.py
+++ b/solution.py
@@ -12,12 +12,14 @@
 LANES = 128
 
 
-def product_kernel(keys, ny, mark, mine, other, *refs):
+def product_kernel(keys, ny, goes_on, before, mine, other, *refs):
     n = len(keys)
     blocks, out, acc = refs[:n], refs[n], refs[n + 1]
     rows, depth = mine.shape
     height = blocks[0].shape[0]
     kb = depth // STEPS
+    if goes_on:
+        out[...] = before[...]
     for k in range(STEPS):
         cut = slice(k * kb, (k + 1) * kb)
         thin = jnp.concatenate([b[:, cut] for b in blocks], axis=0)
@@ -82,23 +84,23 @@
     )(block)
 
 
-def products(keys, ny, mark, mine, other, blocks):
+def products(keys, ny, goes_on, before, mine, other, blocks):
     n = len(blocks)
     rows, depth = mine.shape
     height = blocks[0].shape[0]
     return pl.pallas_call(
-        functools.partial(product_kernel, keys, ny),
-        in_specs=[pl.BlockSpec(memory_space=pl.ANY)] + [pl.BlockSpec(memory_space=pltpu.VMEM)] * (2 + n),
+        functools.partial(product_kernel, keys, ny, goes_on),
+        in_specs=[pl.BlockSpec(memory_space=pltpu.VMEM)] * (3 + n),
         out_specs=pl.BlockSpec(memory_space=pltpu.VMEM),
-        out_shape=jax.ShapeDtypeStruct((2 * n, height * rows // LANES, LANES), jnp.float32),
+        out_shape=jax.ShapeDtypeStruct((4 * ny, height * rows // LANES, LANES), jnp.float32),
         scratch_shapes=[pltpu.VMEM((2, rows, n * height), jnp.float32)],
         compiler_params=pltpu.CompilerParams(vmem_limit_bytes=8 * 1024 * 1024),
         cost_estimate=pl.CostEstimate(
-            flops=4 * n * height * rows * depth,
-            bytes_accessed=2 * (2 * rows + n * height) * depth,
+            flops=4 * n * height * rows * depth if goes_on else 0,
+            bytes_accessed=2 * (2 * rows + n * height) * depth if goes_on else 0,
             transcendentals=0,
         ),
-    )(mark, mine, other, *blocks)
+    )(before, mine, other, *blocks)
 
 
 def body(sizes, amplitudes, integrals, occ_pair, vir_pair):
@@ -130,8 +132,10 @@
 
     held = {(p, s): block for p, plane in enumerate((near, far)) for s, block in plane.items()}
     mine, held[0, 0] = fetch(amplitudes, integrals)
-    keys = list(held)
-    sent = products(keys, ny, mark, mine, other, [held[k] for k in keys])
+    late = [(0, -3), (0, 4), (1, -3), (1, 4)]
+    early = [k for k in held if k not in late]
+    sent = products(early, ny, False, mark, mine, other, [held[k] for k in early])
+    sent = products(late, ny, True, sent, mine, other, [held[k] for k in late])
     got = lax.all_to_all(sent, ("core", "zl", "x"), 0, 0, tiled=True)
     total = got.reshape(2, 2 * ny, -1, LANES).sum(axis=1)
     left, rest = total[:, :height], total[:, height:]

time: 104 us -> 102 us (0.981)
  waiting for transfers between devices: 7.55 us -> 5.02 us
  Pallas kernels: 4.16 us -> 5.24 us
    ppermute x14, waiting for transfers between devices: 7.55 us -> 5.02 us  [hop(): return lax.ppermute(block, ('y', 'core'), pairs)]
    pallas_call x1 -> x2, Pallas kernels: 3.78 us -> 4.85 us  [products(): pl.pallas_call(functools.partial(product_kernel, keys, ny, goes_on), in_s...]
  transfers between devices with their start and end apart: 16 -> 16, of which waited for: 3 -> 3; matrix products, arithmetic and copies ran while one was open for 0% -> 0% of each run, Pallas kernels for 0% -> 3%
where the time goes in v4:
time: 102 us
  starting transfers between devices  65 us (64%)
  blocking collectives  25.1 us (25%)
  Pallas kernels  5.24 us (5%)
  waiting for transfers between devices  5.02 us (5%)
    ppermute x14, starting transfers between devices, hop(): return lax.ppermute(block, ('y', 'core'), pairs)  51.2 us
    all_to_all x1, blocking collectives, body(): got = lax.all_to_all(sent, ('core', 'zl', 'x'), 0, 0, tiled=True)  25.1 us
    ppermute x1, starting transfers between devices, body(): near, far = ({0: integrals}, {0: lax.ppermute(integrals, 'zh', swap)})  10.6 us
    ppermute x14, waiting for transfers between devices, hop(): return lax.ppermute(block, ('y', 'core'), pairs)  5.02 us
    pallas_call x2, Pallas kernels, products(): pl.pallas_call(functools.partial(product_kernel, keys, ny, goes_on), in_s...  4.85 us
    ppermute x1, starting transfers between devices, body(): other = lax.ppermute(amplitudes, 'core', swap)  3.14 us
  transfers between devices with their start and end apart: 16, of which 3 were waited for; matrix products, arithmetic and copies ran while one was open for 0% of the time, Pallas kernels for 3%

profile of v4, /device:TPU:1, one launch (start us, length us, event | category | flops | bytes accessed | tf_op | source)
XLA Modules:
  0.0 101.6 jit_solution(14024023932344410426)
XLA Ops:
  0.0 4.3 %collective-permute-start.3 = (bf16[16,10240]{1,0:T(8,128)(2,1)}, bf16[16,10240]{1,0:T(8,128)(2,1)S(1)}, u32[]{:S(2)}, u32[]{:S(2)}) collective-permute-start(bf16[16,10240]{1,0:T(8,128)(2,1)} %own.1), channel_id=1, source_target_pairs={{0,224},{16,48},{32,0},{48,80},{64,32},{80,112},{96,64},{112,144},... | collective-permute-start | bytes 983048 | tf_op jit(solution)/shard_map/ppermute | solution.py:114
  4.3 10.6 %collective-permute-start = (bf16[16,10240]{1,0:T(8,128)(2,1)}, bf16[16,10240]{1,0:T(8,128)(2,1)S(1)}, u32[]{:S(2)}, u32[]{:S(2)}) collective-permute-start(bf16[16,10240]{1,0:T(8,128)(2,1)} %own.1), channel_id=1, source_target_pairs={{0,256},{256,0},{1,257},{257,1},{2,258},{258,2},{3,259},{259,3},{4... | collective-permute-start | bytes 983048 | tf_op jit(solution)/shard_map/ppermute | solution.py:116
  14.9 3.8 %collective-permute-start.4 = (bf16[16,10240]{1,0:T(8,128)(2,1)}, bf16[16,10240]{1,0:T(8,128)(2,1)S(1)}, u32[]{:S(2)}, u32[]{:S(2)}) collective-permute-start(bf16[16,10240]{1,0:T(8,128)(2,1)} %own.1), channel_id=1, source_target_pairs={{0,32},{16,240},{32,64},{48,16},{64,96},{80,48},{96,128},{112,80},... | collective-permute-start | bytes 983048 | tf_op jit(solution)/shard_map/ppermute | solution.py:114
  18.8 3.1 %collective-permute-start.2 = (bf16[192,10240]{1,0:T(8,128)(2,1)}, bf16[192,10240]{1,0:T(8,128)(2,1)S(1)}, u32[]{:S(2)}, u32[]{:S(2)}) collective-permute-start(bf16[192,10240]{1,0:T(8,128)(2,1)} %mine.1), channel_id=1, source_target_pairs={{0,16},{16,0},{1,17},{17,1},{2,18},{18,2},{3,19},{19,3},{4,20},{20... | collective-permute-start | bytes 11796488 | tf_op jit(solution)/shard_map/ppermute | solution.py:119
  21.9 0.0 collective-permute-done.3.refs_1_
  21.9 1.9 %collective-permute-start.5 = (bf16[16,10240]{1,0:T(8,128)(2,1)S(1)}, bf16[16,10240]{1,0:T(8,128)(2,1)S(1)}, u32[]{:S(2)}, u32[]{:S(2)}) collective-permute-start(bf16[16,10240]{1,0:T(8,128)(2,1)S(1)} %collective-permute-done.3.refs_1_), channel_id=1, source_target_pairs={{0,224},{16,48},{32,0},{48,80},{64,32},{80,112},{96,64},{112,144},... | collective-permute-start | bytes 983048 | tf_op jit(solution)/shard_map/ppermute | solution.py:114
  23.9 3.0 %collective-permute-start.1 = (bf16[16,10240]{1,0:T(8,128)(2,1)S(1)}, bf16[16,10240]{1,0:T(8,128)(2,1)S(1)}, u32[]{:S(2)}, u32[]{:S(2)}) collective-permute-start(bf16[16,10240]{1,0:T(8,128)(2,1)S(1)} %collective-permute-done.block.refs_6_), channel_id=1, source_target_pairs={{0,224},{16,48},{32,0},{48,80},{64,32},{80,112},{96,64},{112,144},... | collective-permute-start | bytes 983048 | tf_op jit(solution)/shard_map/ppermute | solution.py:114
  26.9 3.7 %collective-permute-start.7 = (bf16[16,10240]{1,0:T(8,128)(2,1)S(1)}, bf16[16,10240]{1,0:T(8,128)(2,1)S(1)}, u32[]{:S(2)}, u32[]{:S(2)}) collective-permute-start(bf16[16,10240]{1,0:T(8,128)(2,1)S(1)} %collective-permute-done.4.refs_2_), channel_id=1, source_target_pairs={{0,32},{16,240},{32,64},{48,16},{64,96},{80,48},{96,128},{112,80},... | collective-permute-start | bytes 983048 | tf_op jit(solution)/shard_map/ppermute | solution.py:114
  30.7 0.6 collective-permute-done.5.refs_3_
  31.3 3.6 %collective-permute-start.9 = (bf16[16,10240]{1,0:T(8,128)(2,1)S(1)}, bf16[16,10240]{1,0:T(8,128)(2,1)S(1)}, u32[]{:S(2)}, u32[]{:S(2)}) collective-permute-start(bf16[16,10240]{1,0:T(8,128)(2,1)S(1)} %collective-permute-done.block.refs_6_), channel_id=1, source_target_pairs={{0,32},{16,240},{32,64},{48,16},{64,96},{80,48},{96,128},{112,80},... | collective-permute-start | bytes 983048 | tf_op jit(solution)/shard_map/ppermute | solution.py:114
  34.9 0.0 collective-permute-done.1.refs_7_
  34.9 1.9 %collective-permute-start.6 = (bf16[16,10240]{1,0:T(8,128)(2,1)S(1)}, bf16[16,10240]{1,0:T(8,128)(2,1)S(1)}, u32[]{:S(2)}, u32[]{:S(2)}) collective-permute-start(bf16[16,10240]{1,0:T(8,128)(2,1)S(1)} %collective-permute-done.1.refs_7_), channel_id=1, source_target_pairs={{0,224},{16,48},{32,0},{48,80},{64,32},{80,112},{96,64},{112,144},... | collective-permute-start | bytes 983048 | tf_op jit(solution)/shard_map/ppermute | solution.py:114
  36.8 8.5 %collective-permute-start.8 = (bf16[16,10240]{1,0:T(8,128)(2,1)S(1)}, bf16[16,10240]{1,0:T(8,128)(2,1)S(1)}, u32[]{:S(2)}, u32[]{:S(2)}) collective-permute-start(bf16[16,10240]{1,0:T(8,128)(2,1)S(1)} %collective-permute-done.5.refs_3_), channel_id=1, source_target_pairs={{0,224},{16,48},{32,0},{48,80},{64,32},{80,112},{96,64},{112,144},... | collective-permute-start | bytes 983048 | tf_op jit(solution)/shard_map/ppermute | solution.py:114
  45.3 0.0 collective-permute-done.9.refs_8_
  45.3 1.9 %collective-permute-start.10 = (bf16[16,10240]{1,0:T(8,128)(2,1)S(1)}, bf16[16,10240]{1,0:T(8,128)(2,1)S(1)}, u32[]{:S(2)}, u32[]{:S(2)}) collective-permute-start(bf16[16,10240]{1,0:T(8,128)(2,1)S(1)} %collective-permute-done.9.refs_8_), channel_id=1, source_target_pairs={{0,32},{16,240},{32,64},{48,16},{64,96},{80,48},{96,128},{112,80},... | collective-permute-start | bytes 983048 | tf_op jit(solution)/shard_map/ppermute | solution.py:114
  47.3 0.0 collective-permute-done.6.refs_9_
  47.3 5.0 %collective-permute-start.11 = (bf16[16,10240]{1,0:T(8,128)(2,1)S(1)}, bf16[16,10240]{1,0:T(8,128)(2,1)S(1)}, u32[]{:S(2)}, u32[]{:S(2)}) collective-permute-start(bf16[16,10240]{1,0:T(8,128)(2,1)S(1)} %collective-permute-done.6.refs_9_), channel_id=1, source_target_pairs={{0,224},{16,48},{32,0},{48,80},{64,32},{80,112},{96,64},{112,144},... | collective-permute-start | bytes 983048 | tf_op jit(solution)/shard_map/ppermute | solution.py:114
  52.3 1.9 %collective-permute-start.12 = (bf16[16,10240]{1,0:T(8,128)(2,1)S(1)}, bf16[16,10240]{1,0:T(8,128)(2,1)S(1)}, u32[]{:S(2)}, u32[]{:S(2)}) collective-permute-start(bf16[16,10240]{1,0:T(8,128)(2,1)S(1)} %collective-permute-done.7.refs_4_), channel_id=1, source_target_pairs={{0,32},{16,240},{32,64},{48,16},{64,96},{80,48},{96,128},{112,80},... | collective-permute-start | bytes 983048 | tf_op jit(solution)/shard_map/ppermute | solution.py:114
  54.2 0.0 collective-permute-done.8.refs_5_
  54.2 5.3 %collective-permute-start.13 = (bf16[16,10240]{1,0:T(8,128)(2,1)S(1)}, bf16[16,10240]{1,0:T(8,128)(2,1)S(1)}, u32[]{:S(2)}, u32[]{:S(2)}) collective-permute-start(bf16[16,10240]{1,0:T(8,128)(2,1)S(1)} %collective-permute-done.8.refs_5_), channel_id=1, source_target_pairs={{0,224},{16,48},{32,0},{48,80},{64,32},{80,112},{96,64},{112,144},... | collective-permute-start | bytes 983048 | tf_op jit(solution)/shard_map/ppermute | solution.py:114
  59.6 1.9 %collective-permute-start.14 = (bf16[16,10240]{1,0:T(8,128)(2,1)S(1)}, bf16[16,10240]{1,0:T(8,128)(2,1)S(1)}, u32[]{:S(2)}, u32[]{:S(2)}) collective-permute-start(bf16[16,10240]{1,0:T(8,128)(2,1)S(1)} %collective-permute-done.10.refs_10_), channel_id=1, source_target_pairs={{0,32},{16,240},{32,64},{48,16},{64,96},{80,48},{96,128},{112,80},... | collective-permute-start | bytes 983048 | tf_op jit(solution)/shard_map/ppermute | solution.py:114
  61.5 4.3 %collective-permute-start.15 = (bf16[16,10240]{1,0:T(8,128)(2,1)S(1)}, bf16[16,10240]{1,0:T(8,128)(2,1)S(1)}, u32[]{:S(2)}, u32[]{:S(2)}) collective-permute-start(bf16[16,10240]{1,0:T(8,128)(2,1)S(1)} %collective-permute-done.11.refs_11_), channel_id=1, source_target_pairs={{0,224},{16,48},{32,0},{48,80},{64,32},{80,112},{96,64},{112,144},... | collective-permute-start | bytes 983048 | tf_op jit(solution)/shard_map/ppermute | solution.py:114
  65.9 0.4 shard_map.47
  66.3 2.5 %shard_map.48.before = f32[32,24,128]{2,1,0:T(8,128)S(1)} custom-call(s32[8,128]{1,0:T(8,128)S(1)} %shard_map.46.before, bf16[192,10240]{1,0:T(8,128)(2,1)S(1)} %get-tuple-element.16.mine, bf16[192,10240]{1,0:T(8,128)(2,1)S(1)} %collective-permute-done.2.other, bf16[16,10240]{1,0:T(8,128)(2,1)S(1)} %get-tuple-element.19.refs_0_, ...), custom_call_target="tpu_custom_call" | custom-call | tf_op jit(solution)/shard_map/pallas_call | solution.py:91
  68.8 0.0 copy-start.2
  68.8 0.0 copy-start.3
  68.8 2.7 %collective-permute-done.14.refs_2_ = bf16[16,10240]{1,0:T(8,128)(2,1)S(1)} collective-permute-done((bf16[16,10240]{1,0:T(8,128)(2,1)S(1)}, bf16[16,10240]{1,0:T(8,128)(2,1)S(1)}, u32[]{:S(2)}, u32[]{:S(2)}) %collective-permute-start.14) | collective-permute-done | bytes 327712 | tf_op jit(solution)/shard_map/ppermute | solution.py:114
  71.6 1.7 %collective-permute-done.15.refs_3_ = bf16[16,10240]{1,0:T(8,128)(2,1)S(1)} collective-permute-done((bf16[16,10240]{1,0:T(8,128)(2,1)S(1)}, bf16[16,10240]{1,0:T(8,128)(2,1)S(1)}, u32[]{:S(2)}, u32[]{:S(2)}) %collective-permute-start.15) | collective-permute-done | bytes 327712 | tf_op jit(solution)/shard_map/ppermute | solution.py:114
  73.2 2.4 %shard_map.49 = f32[32,24,128]{2,1,0:T(8,128)S(1)} custom-call(f32[32,24,128]{2,1,0:T(8,128)S(1)} %shard_map.48.before, bf16[192,10240]{1,0:T(8,128)(2,1)S(1)} %get-tuple-element.16.mine, bf16[192,10240]{1,0:T(8,128)(2,1)S(1)} %collective-permute-done.2.other, bf16[16,10240]{1,0:T(8,128)(2,1)S(1)} %collective-permute-done.12.refs_0_, ...), custom_call_target="tpu_custom_call" | custom-call | flops 503316480 | bytes 9175040 | tf_op jit(solution)/shard_map/pallas_call | solution.py:91
  75.6 25.1 %all_to_all.5 = f32[32,24,128]{2,1,0:T(8,128)S(1)} all-to-all(f32[32,24,128]{2,1,0:T(8,128)S(1)} %shard_map.49), channel_id=1, replica_groups=mesh['zh'=2,'y'=8,'core'=2,'zl'=4,'x'=4] {'core','zl','x'}, dimensions={0} | all-to-all | bytes 786432 | tf_op jit(solution)/shard_map/all_to_all | solution.py:139
  100.7 0.1 fusion
  100.9 0.7 bitcast_divide_fusion
  (18 shorter events, 0.1 us)
Async XLA Ops:
  0.0 65.9 %copy-start.1 = (bf16[16,10240]{1,0:T(8,128)(2,1)S(1)}, bf16[16,10240]{1,0:T(8,128)(2,1)}, u32[]{:S(2)}) copy-start(bf16[16,10240]{1,0:T(8,128)(2,1)} %own.1) | copy-start | bytes 983044
  0.0 65.9 %copy-start = (bf16[192,10240]{1,0:T(8,128)(2,1)S(1)}, bf16[192,10240]{1,0:T(8,128)(2,1)}, u32[]{:S(2)}) copy-start(bf16[192,10240]{1,0:T(8,128)(2,1)} %mine.1) | copy-start | bytes 11796484
  0.0 21.9 %collective-permute-start.3 = (bf16[16,10240]{1,0:T(8,128)(2,1)}, bf16[16,10240]{1,0:T(8,128)(2,1)S(1)}, u32[]{:S(2)}, u32[]{:S(2)}) collective-permute-start(bf16[16,10240]{1,0:T(8,128)(2,1)} %own.1), channel_id=1, source_target_pairs={{0,224},{16,48},{32,0},{48,80},{64,32},{80,112},{96,64},{112,144},... | collective-permute-start | bytes 983048 | tf_op jit(solution)/shard_map/ppermute | solution.py:114
  4.3 19.6 %collective-permute-start = (bf16[16,10240]{1,0:T(8,128)(2,1)}, bf16[16,10240]{1,0:T(8,128)(2,1)S(1)}, u32[]{:S(2)}, u32[]{:S(2)}) collective-permute-start(bf16[16,10240]{1,0:T(8,128)(2,1)} %own.1), channel_id=1, source_target_pairs={{0,256},{256,0},{1,257},{257,1},{2,258},{258,2},{3,259},{259,3},{4... | collective-permute-start | bytes 983048 | tf_op jit(solution)/shard_map/ppermute | solution.py:116
  14.9 12.0 %collective-permute-start.4 = (bf16[16,10240]{1,0:T(8,128)(2,1)}, bf16[16,10240]{1,0:T(8,128)(2,1)S(1)}, u32[]{:S(2)}, u32[]{:S(2)}) collective-permute-start(bf16[16,10240]{1,0:T(8,128)(2,1)} %own.1), channel_id=1, source_target_pairs={{0,32},{16,240},{32,64},{48,16},{64,96},{80,48},{96,128},{112,80},... | collective-permute-start | bytes 983048 | tf_op jit(solution)/shard_map/ppermute | solution.py:114
  18.8 16.1 %collective-permute-start.2 = (bf16[192,10240]{1,0:T(8,128)(2,1)}, bf16[192,10240]{1,0:T(8,128)(2,1)S(1)}, u32[]{:S(2)}, u32[]{:S(2)}) collective-permute-start(bf16[192,10240]{1,0:T(8,128)(2,1)} %mine.1), channel_id=1, source_target_pairs={{0,16},{16,0},{1,17},{17,1},{2,18},{18,2},{3,19},{19,3},{4,20},{20... | collective-permute-start | bytes 11796488 | tf_op jit(solution)/shard_map/ppermute | solution.py:119
  21.9 9.4 %collective-permute-start.5 = (bf16[16,10240]{1,0:T(8,128)(2,1)S(1)}, bf16[16,10240]{1,0:T(8,128)(2,1)S(1)}, u32[]{:S(2)}, u32[]{:S(2)}) collective-permute-start(bf16[16,10240]{1,0:T(8,128)(2,1)S(1)} %collective-permute-done.3.refs_1_), channel_id=1, source_target_pairs={{0,224},{16,48},{32,0},{48,80},{64,32},{80,112},{96,64},{112,144},... | collective-permute-start | bytes 983048 | tf_op jit(solution)/shard_map/ppermute | solution.py:114
  23.9 11.0 %collective-permute-start.1 = (bf16[16,10240]{1,0:T(8,128)(2,1)S(1)}, bf16[16,10240]{1,0:T(8,128)(2,1)S(1)}, u32[]{:S(2)}, u32[]{:S(2)}) collective-permute-start(bf16[16,10240]{1,0:T(8,128)(2,1)S(1)} %collective-permute-done.block.refs_6_), channel_id=1, source_target_pairs={{0,224},{16,48},{32,0},{48,80},{64,32},{80,112},{96,64},{112,144},... | collective-permute-start | bytes 983048 | tf_op jit(solution)/shard_map/ppermute | solution.py:114
  26.9 20.3 %collective-permute-start.7 = (bf16[16,10240]{1,0:T(8,128)(2,1)S(1)}, bf16[16,10240]{1,0:T(8,128)(2,1)S(1)}, u32[]{:S(2)}, u32[]{:S(2)}) collective-permute-start(bf16[16,10240]{1,0:T(8,128)(2,1)S(1)} %collective-permute-done.4.refs_2_), channel_id=1, source_target_pairs={{0,32},{16,240},{32,64},{48,16},{64,96},{80,48},{96,128},{112,80},... | collective-permute-start | bytes 983048 | tf_op jit(solution)/shard_map/ppermute | solution.py:114
  31.3 14.0 %collective-permute-start.9 = (bf16[16,10240]{1,0:T(8,128)(2,1)S(1)}, bf16[16,10240]{1,0:T(8,128)(2,1)S(1)}, u32[]{:S(2)}, u32[]{:S(2)}) collective-permute-start(bf16[16,10240]{1,0:T(8,128)(2,1)S(1)} %collective-permute-done.block.refs_6_), channel_id=1, source_target_pairs={{0,32},{16,240},{32,64},{48,16},{64,96},{80,48},{96,128},{112,80},... | collective-permute-start | bytes 983048 | tf_op jit(solution)/shard_map/ppermute | solution.py:114
  34.9 12.4 %collective-permute-start.6 = (bf16[16,10240]{1,0:T(8,128)(2,1)S(1)}, bf16[16,10240]{1,0:T(8,128)(2,1)S(1)}, u32[]{:S(2)}, u32[]{:S(2)}) collective-permute-start(bf16[16,10240]{1,0:T(8,128)(2,1)S(1)} %collective-permute-done.1.refs_7_), channel_id=1, source_target_pairs={{0,224},{16,48},{32,0},{48,80},{64,32},{80,112},{96,64},{112,144},... | collective-permute-start | bytes 983048 | tf_op jit(solution)/shard_map/ppermute | solution.py:114
  36.8 17.4 %collective-permute-start.8 = (bf16[16,10240]{1,0:T(8,128)(2,1)S(1)}, bf16[16,10240]{1,0:T(8,128)(2,1)S(1)}, u32[]{:S(2)}, u32[]{:S(2)}) collective-permute-start(bf16[16,10240]{1,0:T(8,128)(2,1)S(1)} %collective-permute-done.5.refs_3_), channel_id=1, source_target_pairs={{0,224},{16,48},{32,0},{48,80},{64,32},{80,112},{96,64},{112,144},... | collective-permute-start | bytes 983048 | tf_op jit(solution)/shard_map/ppermute | solution.py:114
  45.3 14.3 %collective-permute-start.10 = (bf16[16,10240]{1,0:T(8,128)(2,1)S(1)}, bf16[16,10240]{1,0:T(8,128)(2,1)S(1)}, u32[]{:S(2)}, u32[]{:S(2)}) collective-permute-start(bf16[16,10240]{1,0:T(8,128)(2,1)S(1)} %collective-permute-done.9.refs_8_), channel_id=1, source_target_pairs={{0,32},{16,240},{32,64},{48,16},{64,96},{80,48},{96,128},{112,80},... | collective-permute-start | bytes 983048 | tf_op jit(solution)/shard_map/ppermute | solution.py:114
  47.3 14.3 %collective-permute-start.11 = (bf16[16,10240]{1,0:T(8,128)(2,1)S(1)}, bf16[16,10240]{1,0:T(8,128)(2,1)S(1)}, u32[]{:S(2)}, u32[]{:S(2)}) collective-permute-start(bf16[16,10240]{1,0:T(8,128)(2,1)S(1)} %collective-permute-done.6.refs_9_), channel_id=1, source_target_pairs={{0,224},{16,48},{32,0},{48,80},{64,32},{80,112},{96,64},{112,144},... | collective-permute-start | bytes 983048 | tf_op jit(solution)/shard_map/ppermute | solution.py:114
  52.3 16.5 %collective-permute-start.12 = (bf16[16,10240]{1,0:T(8,128)(2,1)S(1)}, bf16[16,10240]{1,0:T(8,128)(2,1)S(1)}, u32[]{:S(2)}, u32[]{:S(2)}) collective-permute-start(bf16[16,10240]{1,0:T(8,128)(2,1)S(1)} %collective-permute-done.7.refs_4_), channel_id=1, source_target_pairs={{0,32},{16,240},{32,64},{48,16},{64,96},{80,48},{96,128},{112,80},... | collective-permute-start | bytes 983048 | tf_op jit(solution)/shard_map/ppermute | solution.py:114
  54.2 14.6 %collective-permute-start.13 = (bf16[16,10240]{1,0:T(8,128)(2,1)S(1)}, bf16[16,10240]{1,0:T(8,128)(2,1)S(1)}, u32[]{:S(2)}, u32[]{:S(2)}) collective-permute-start(bf16[16,10240]{1,0:T(8,128)(2,1)S(1)} %collective-permute-done.8.refs_5_), channel_id=1, source_target_pairs={{0,224},{16,48},{32,0},{48,80},{64,32},{80,112},{96,64},{112,144},... | collective-permute-start | bytes 983048 | tf_op jit(solution)/shard_map/ppermute | solution.py:114
  59.6 12.0 %collective-permute-start.14 = (bf16[16,10240]{1,0:T(8,128)(2,1)S(1)}, bf16[16,10240]{1,0:T(8,128)(2,1)S(1)}, u32[]{:S(2)}, u32[]{:S(2)}) collective-permute-start(bf16[16,10240]{1,0:T(8,128)(2,1)S(1)} %collective-permute-done.10.refs_10_), channel_id=1, source_target_pairs={{0,32},{16,240},{32,64},{48,16},{64,96},{80,48},{96,128},{112,80},... | collective-permute-start | bytes 983048 | tf_op jit(solution)/shard_map/ppermute | solution.py:114
  61.5 11.7 %collective-permute-start.15 = (bf16[16,10240]{1,0:T(8,128)(2,1)S(1)}, bf16[16,10240]{1,0:T(8,128)(2,1)S(1)}, u32[]{:S(2)}, u32[]{:S(2)}) collective-permute-start(bf16[16,10240]{1,0:T(8,128)(2,1)S(1)} %collective-permute-done.11.refs_11_), channel_id=1, source_target_pairs={{0,224},{16,48},{32,0},{48,80},{64,32},{80,112},{96,64},{112,144},... | collective-permute-start | bytes 983048 | tf_op jit(solution)/shard_map/ppermute | solution.py:114
  68.8 32.0 %copy-start.2 = (f32[192]{0:T(256)S(1)}, f32[192]{0:T(256)}, u32[]{:S(2)}) copy-start(f32[192]{0:T(256)} %param.6) | copy-start | bytes 2308
  68.8 32.0 %copy-start.3 = (f32[32]{0:T(128)S(1)}, f32[32]{0:T(128)}, u32[]{:S(2)}) copy-start(f32[32]{0:T(128)} %param.7) | copy-start | bytes 388
